TPU v7x, 32 devices: a whole 2x2x4 slice. The times are simulated.
32 devices in a mesh: ctx: 16 (over z, x, core), fsdp: 2 (over y).
Axes of the slice: x: 2, y: 2, z: 4, core: 2. Of those that a mesh axis runs over, the one named last changes fastest.
Arguments:
- tokens: bfloat16 [4, 1024, 576], P('fsdp', 'ctx'), may hold values from -6 to 6
- query_matrix: bfloat16 [576, 576], P('fsdp'), may hold values from -0.25 to 0.25
- key_projection: bfloat16 [576, 192], P('fsdp'), may hold values from -0.25 to 0.25
- value_projection: bfloat16 [576, 192], P('fsdp'), may hold values from -0.25 to 0.25
- output_matrix: bfloat16 [576, 576], P('fsdp'), may hold values from -2 to 2
- attn_gain: bfloat16 [576], P('fsdp'), may hold values from 0.099609375 to 1.8984375
- mlp_gain: bfloat16 [576], P('fsdp'), may hold values from 0.099609375 to 1.8984375
- gate_matrix: bfloat16 [576, 1536], P(None, 'fsdp'), may hold values from -0.25 to 0.25
- up_matrix: bfloat16 [576, 1536], P(None, 'fsdp'), may hold values from -0.25 to 0.25
- down_matrix: bfloat16 [1536, 576], P('fsdp'), may hold values from -0.15625 to 0.15625
- pair_table: int32 [16, 2], replicated, may hold values from 0 to 31, as said below
- doc_ids: int32 [4, 1024], P('fsdp'), may hold values from 0 to 15, never falling along the last dimension, each value on 1 to 128 neighbouring positions
- out_grad: bfloat16 [4, 1024, 576], P('fsdp', 'ctx'), may hold values from -6 to 6
Outputs:
- block_out: bfloat16 [4, 1024, 576], P('fsdp', 'ctx')
- input_grad: float32 [4, 1024, 576], P('fsdp', 'ctx')
- query_grad: float32 [576, 576], P('fsdp')
- key_grad: float32 [576, 192], P('fsdp')
- value_grad: float32 [576, 192], P('fsdp')
- output_grad: float32 [576, 576], P('fsdp')
- attn_gain_grad: float32 [576], P('fsdp')
- mlp_gain_grad: float32 [576], P('fsdp')
- gate_grad: float32 [576, 1536], P(None, 'fsdp')
- up_grad: float32 [576, 1536], P(None, 'fsdp')
- down_grad: float32 [1536, 576], P('fsdp')
Inputs may be any that keep to these rules, and one draw needn't show every extreme that they name: `pair_table`: row i holds a block number b below 16 and then its mirror 2 * 16 - 1 - b; the first entries of the rows are each of 0 to 15 once. `doc_ids`: document ids never fall along a sequence; every id of 0 to 15 appears, each document holds 1 to 128 positions, and one holds exactly 128.
All inputs are finite; a program needn't handle non-finite values.
Results may differ from a plain program's by a relative error of at most 0.02.
Values may be sent and summed in bfloat16 or wider, within the bound.
A program may use at most 192 MiB of HBM per device.

v0:
```python
import math

import jax
import jax.numpy as jnp
from jax import lax
from jax.sharding import PartitionSpec as P

QUERY_HEADS = 9
KEY_VALUE_HEADS = 3
HEAD_SIZE = 64


epsilon = 1e-05
theta_base = 10000.0
masked_logits = -1e30


def rope_tables(token_positions):
    half = HEAD_SIZE // 2
    freq = theta_base ** (-jnp.arange(half, dtype=jnp.float32) * 2.0 / HEAD_SIZE)
    angles = token_positions.astype(jnp.float32)[:, None] * freq[None, :]
    cosine_table = jnp.concatenate([jnp.cos(angles), jnp.cos(angles)], axis=-1)
    sine_table = jnp.concatenate([jnp.sin(angles), jnp.sin(angles)], axis=-1)
    return (cosine_table[:, None, :], sine_table[:, None, :])


def rotary_apply(value_rows, cosine_table, sine_table):
    half = value_rows.shape[-1] // 2
    turned = jnp.concatenate([-value_rows[..., half:], value_rows[..., :half]], axis=-1)
    return value_rows * cosine_table + turned * sine_table


def rotary_inverse(grads, cosine_table, sine_table):
    half = grads.shape[-1] // 2
    scaled = grads * sine_table
    turned = jnp.concatenate([scaled[..., half:], -scaled[..., :half]], axis=-1)
    return grads * cosine_table + turned


def normalize(value_rows):
    inverse = lax.rsqrt(jnp.mean(value_rows * value_rows, axis=-1, keepdims=True) + epsilon)
    return (inverse, value_rows * inverse)


def rms_back(grads, inverse, normed):
    return inverse * (grads - normed * jnp.mean(grads * normed, axis=-1, keepdims=True))


def outer_sum(left, right):
    flat_left = left.reshape(-1, left.shape[-1])
    flat_right = right.reshape(-1, right.shape[-1])
    return lax.dot_general(
        flat_left, flat_right, (((0,), (0,)), ((), ())), preferred_element_type=jnp.float32
    )


def back_dot(grads, weight):
    return lax.dot_general(
        grads, weight, (((grads.ndim - 1,), (1,)), ((), ())), preferred_element_type=jnp.float32
    )


def allowed_mask(start_offset, key_increment, query_pos, query_doc, key_doc):
    key_pos = start_offset + jnp.arange(key_increment, dtype=jnp.int32)
    causal = key_pos[None, :] <= query_pos[:, None]
    same = key_doc[:, None, :] == query_doc[:, :, None]
    return (causal[None] & same)[:, None, None]


def key_slices(
    key_blocks, value_blocks, doc_ids, where_dealt, start_offset, key_increment, block_index
):
    sequence_group = key_blocks.shape[0]
    per_tile = key_increment // block_index
    slots = lax.dynamic_slice_in_dim(where_dealt, start_offset // block_index, per_tile, 0)
    key_rows = jnp.take(key_blocks, slots, axis=1).reshape(
        sequence_group, key_increment, KEY_VALUE_HEADS, HEAD_SIZE
    )
    value_rows = jnp.take(value_blocks, slots, axis=1).reshape(
        sequence_group, key_increment, KEY_VALUE_HEADS, HEAD_SIZE
    )
    key_doc = lax.dynamic_slice_in_dim(doc_ids, start_offset, key_increment, 1)
    return (key_rows, value_rows, key_doc, slots)


def attend_half(
    query,
    key_blocks,
    value_blocks,
    where_dealt,
    doc_ids,
    query_pos,
    query_doc,
    first_block,
    first_tile,
    block_index,
    key_increment,
):
    sequence_group = query.shape[0]
    group_index = QUERY_HEADS // KEY_VALUE_HEADS
    scale = 1.0 / math.sqrt(HEAD_SIZE)
    count = ((first_block + 1) * block_index + key_increment - 1) // key_increment

    def step(index, carry):
        top, total, accum = carry
        start_offset = index * key_increment
        key_rows, value_rows, key_doc, slots = key_slices(
            key_blocks, value_blocks, doc_ids, where_dealt, start_offset, key_increment, block_index
        )
        allowed = allowed_mask(start_offset, key_increment, query_pos, query_doc, key_doc)
        scores = (
            jnp.einsum("sqhgd,skhd->shgqk", query, key_rows, preferred_element_type=jnp.float32)
            * scale
        )
        scores = jnp.where(allowed, scores, masked_logits)
        new_top = jnp.maximum(top, jnp.max(scores, axis=-1))
        weights = jnp.where(allowed, jnp.exp(scores - new_top[..., None]), 0.0)
        shrink = jnp.exp(top - new_top)
        total = total * shrink + jnp.sum(weights, axis=-1)
        accum = accum * shrink[..., None] + jnp.einsum(
            "shgqk,skhd->shgqd",
            weights.astype(jnp.bfloat16),
            value_rows,
            preferred_element_type=jnp.float32,
        )
        return (new_top, total, accum)

    start_upper_bound = jnp.full(
        (sequence_group, KEY_VALUE_HEADS, group_index, block_index), masked_logits, jnp.float32
    )
    start_overall = jnp.zeros(
        (sequence_group, KEY_VALUE_HEADS, group_index, block_index), jnp.float32
    )
    start_accumulate = jnp.zeros(
        (sequence_group, KEY_VALUE_HEADS, group_index, block_index, HEAD_SIZE), jnp.float32
    )
    top, total, accum = lax.fori_loop(
        first_tile, count, step, (start_upper_bound, start_overall, start_accumulate)
    )
    result = accum / total[..., None]
    return (jnp.transpose(result, (0, 3, 1, 2, 4)), top + jnp.log(total))


def attend_back(
    query,
    key_blocks,
    value_blocks,
    where_dealt,
    doc_ids,
    query_pos,
    query_doc,
    first_block,
    first_tile,
    block_index,
    key_increment,
    grad_half,
    log_total,
    delta,
    key_accumulator,
    value_accumulator,
):
    sequence_group = query.shape[0]
    group_index = QUERY_HEADS // KEY_VALUE_HEADS
    scale = 1.0 / math.sqrt(HEAD_SIZE)
    per_tile = key_increment // block_index
    count = ((first_block + 1) * block_index + key_increment - 1) // key_increment

    def step(index, carry):
        query_acc, key_running_sum, value_running_sum = carry
        start_offset = index * key_increment
        key_rows, value_rows, key_doc, slots = key_slices(
            key_blocks, value_blocks, doc_ids, where_dealt, start_offset, key_increment, block_index
        )
        allowed = allowed_mask(start_offset, key_increment, query_pos, query_doc, key_doc)
        scores = (
            jnp.einsum("sqhgd,skhd->shgqk", query, key_rows, preferred_element_type=jnp.float32)
            * scale
        )
        probs = jnp.where(allowed, jnp.exp(scores - log_total[..., None]), 0.0)
        value_portion = jnp.einsum(
            "shgqk,sqhgd->skhd",
            probs.astype(jnp.bfloat16),
            grad_half,
            preferred_element_type=jnp.float32,
        )
        prob_grad = jnp.einsum(
            "sqhgd,skhd->shgqk", grad_half, value_rows, preferred_element_type=jnp.float32
        )
        score_grad = (probs * (prob_grad - delta[..., None])).astype(jnp.bfloat16)
        query_acc = (
            query_acc
            + jnp.einsum(
                "shgqk,skhd->sqhgd", score_grad, key_rows, preferred_element_type=jnp.float32
            )
            * scale
        )
        key_portion = (
            jnp.einsum("shgqk,sqhgd->skhd", score_grad, query, preferred_element_type=jnp.float32)
            * scale
        )
        key_running_sum = key_running_sum.at[:, slots].add(
            key_portion.reshape(sequence_group, per_tile, block_index, KEY_VALUE_HEADS * HEAD_SIZE)
        )
        value_running_sum = value_running_sum.at[:, slots].add(
            value_portion.reshape(
                sequence_group, per_tile, block_index, KEY_VALUE_HEADS * HEAD_SIZE
            )
        )
        return (query_acc, key_running_sum, value_running_sum)

    query_start_offset = jnp.zeros(
        (sequence_group, block_index, KEY_VALUE_HEADS, group_index, HEAD_SIZE), jnp.float32
    )
    return lax.fori_loop(
        first_tile, count, step, (query_start_offset, key_accumulator, value_accumulator)
    )


def feed_forward(hidden_rows, grad_rows, gate_weight, up_weight, down_weight):
    gate = jnp.dot(hidden_rows, gate_weight, preferred_element_type=jnp.float32)
    upper = jnp.dot(hidden_rows, up_weight, preferred_element_type=jnp.float32)
    sigma = jax.nn.sigmoid(gate)
    activated = (gate * sigma * upper).astype(jnp.bfloat16)
    branch_out = jnp.dot(activated, down_weight, preferred_element_type=jnp.float32)
    down_wgrad = outer_sum(activated, grad_rows)
    act_grad = back_dot(grad_rows, down_weight)
    up_grad_r = (act_grad * gate * sigma).astype(jnp.bfloat16)
    gate_grad_r = (act_grad * upper * sigma * (1.0 + gate * (1.0 - sigma))).astype(jnp.bfloat16)
    gate_wgrad = outer_sum(hidden_rows, gate_grad_r)
    up_wgrad = outer_sum(hidden_rows, up_grad_r)
    hidden_grad = back_dot(gate_grad_r, gate_weight) + back_dot(up_grad_r, up_weight)
    return (branch_out, hidden_grad, gate_wgrad, up_wgrad, down_wgrad)


def body(
    tokens,
    query_matrix,
    key_projection,
    value_projection,
    output_matrix,
    attn_gain,
    mlp_gain,
    gate_matrix,
    up_matrix,
    down_matrix,
    pair_table,
    doc_ids,
    out_grad,
):
    sequence_group, token_per_shard, width = tokens.shape
    pairs = lax.axis_size("ctx")
    block_index = token_per_shard // 2
    length_value = token_per_shard * pairs
    blocks = 2 * pairs
    group_index = QUERY_HEADS // KEY_VALUE_HEADS
    per_tile = math.gcd(max(1, 256 // block_index), blocks)
    key_increment = per_tile * block_index
    kv_width = KEY_VALUE_HEADS * HEAD_SIZE
    query_full, key_full, value_full, output_full, attn_scale, mlp_scale = (
        lax.all_gather(query_matrix, "fsdp", axis=0, tiled=True),
        lax.all_gather(key_projection, "fsdp", axis=0, tiled=True),
        lax.all_gather(value_projection, "fsdp", axis=0, tiled=True),
        lax.all_gather(output_matrix, "fsdp", axis=0, tiled=True),
        lax.all_gather(attn_gain, "fsdp", axis=0, tiled=True),
        lax.all_gather(mlp_gain, "fsdp", axis=0, tiled=True),
    )
    table_row = lax.dynamic_index_in_dim(pair_table, lax.axis_index("ctx"), 0, keepdims=False)
    local = jnp.arange(token_per_shard, dtype=jnp.int32)
    own_pos = (
        jnp.where(local < block_index, table_row[0], table_row[1]) * block_index
        + local % block_index
    )
    query_doc = jnp.take(doc_ids, own_pos, axis=1)
    cosine_table, sine_table = rope_tables(own_pos)
    inputs = tokens.astype(jnp.float32)
    inv_one, normed_one = normalize(inputs)
    attn_gain_f = attn_scale.astype(jnp.float32)
    hidden_one = (normed_one * attn_gain_f).astype(jnp.bfloat16)
    query_lin = jnp.dot(hidden_one, query_full, preferred_element_type=jnp.float32).reshape(
        sequence_group, token_per_shard, QUERY_HEADS, HEAD_SIZE
    )
    key_linear = jnp.dot(hidden_one, key_full, preferred_element_type=jnp.float32).reshape(
        sequence_group, token_per_shard, KEY_VALUE_HEADS, HEAD_SIZE
    )
    value_rows = jnp.dot(hidden_one, value_full, preferred_element_type=jnp.float32).astype(
        jnp.bfloat16
    )
    query_rows = rotary_apply(query_lin, cosine_table, sine_table).astype(jnp.bfloat16)
    key_rows = (
        rotary_apply(key_linear, cosine_table, sine_table)
        .astype(jnp.bfloat16)
        .reshape(sequence_group, token_per_shard, kv_width)
    )
    key_dealt, value_dealt = (
        lax.all_gather(key_rows, "ctx", axis=1, tiled=True),
        lax.all_gather(value_rows, "ctx", axis=1, tiled=True),
    )
    flat_table = pair_table.reshape(-1)
    block_ids = jnp.arange(blocks, dtype=jnp.int32)
    where_dealt = jnp.sum(
        block_ids[None, :] * (flat_table[None, :] == block_ids[:, None]).astype(jnp.int32), axis=1
    )
    key_blocks = key_dealt.reshape(sequence_group, blocks, block_index, kv_width)
    value_blocks = value_dealt.reshape(sequence_group, blocks, block_index, kv_width)
    first_tiles = []
    for half in range(2):
        first_doc = query_doc[:, half * block_index]
        doc_start = jnp.sum((doc_ids < first_doc[:, None]).astype(jnp.int32), axis=1)
        first_tiles.append(jnp.min(doc_start) // key_increment)
    query_group_list = query_rows.reshape(
        sequence_group, token_per_shard, KEY_VALUE_HEADS, group_index, HEAD_SIZE
    )
    halves_out = []
    halves_lse = []
    for half in range(2):
        rows_low = half * block_index
        part_out, part_lse = attend_half(
            query_group_list[:, rows_low : rows_low + block_index],
            key_blocks,
            value_blocks,
            where_dealt,
            doc_ids,
            own_pos[rows_low : rows_low + block_index],
            query_doc[:, rows_low : rows_low + block_index],
            table_row[half],
            first_tiles[half],
            block_index,
            key_increment,
        )
        halves_out.append(part_out)
        halves_lse.append(part_lse)
    attn_out = jnp.concatenate(halves_out, axis=1)
    attn_in = attn_out.reshape(sequence_group, token_per_shard, QUERY_HEADS * HEAD_SIZE).astype(
        jnp.bfloat16
    )
    mixed_heads = inputs + jnp.dot(attn_in, output_full, preferred_element_type=jnp.float32)
    inv_two, normed_two = normalize(mixed_heads)
    mlp_gain_f = mlp_scale.astype(jnp.float32)
    hidden_two = (normed_two * mlp_gain_f).astype(jnp.bfloat16)
    gate_full, up_full, down_full = (
        lax.all_gather(gate_matrix, "fsdp", axis=1, tiled=True),
        lax.all_gather(up_matrix, "fsdp", axis=1, tiled=True),
        lax.all_gather(down_matrix, "fsdp", axis=0, tiled=True),
    )
    branch_out, hidden_two_grad, gate_wgrad, up_wgrad, down_wgrad = feed_forward(
        hidden_two, out_grad, gate_full, up_full, down_full
    )
    block_out = (mixed_heads + branch_out).astype(jnp.bfloat16)
    mlp_gain_wgrad = jnp.sum(hidden_two_grad * normed_two, axis=(0, 1))
    mixed_grad = out_grad.astype(jnp.float32) + rms_back(
        hidden_two_grad * mlp_gain_f, inv_two, normed_two
    )
    branch_grad = mixed_grad.astype(jnp.bfloat16)
    output_wgrad = outer_sum(attn_in, branch_grad)
    attn_grad = (
        back_dot(branch_grad, output_full)
        .astype(jnp.bfloat16)
        .reshape(sequence_group, token_per_shard, KEY_VALUE_HEADS, group_index, HEAD_SIZE)
    )
    key_accumulator = jnp.zeros((sequence_group, blocks, block_index, kv_width), jnp.float32)
    value_accumulator = jnp.zeros((sequence_group, blocks, block_index, kv_width), jnp.float32)
    query_parts = []
    for half in range(2):
        rows_low = half * block_index
        grad_half = attn_grad[:, rows_low : rows_low + block_index]
        delta = jnp.transpose(
            jnp.sum(grad_half.astype(jnp.float32) * halves_out[half], axis=-1), (0, 2, 3, 1)
        )
        part_grad, key_accumulator, value_accumulator = attend_back(
            query_group_list[:, rows_low : rows_low + block_index],
            key_blocks,
            value_blocks,
            where_dealt,
            doc_ids,
            own_pos[rows_low : rows_low + block_index],
            query_doc[:, rows_low : rows_low + block_index],
            table_row[half],
            first_tiles[half],
            block_index,
            key_increment,
            grad_half,
            halves_lse[half],
            delta,
            key_accumulator,
            value_accumulator,
        )
        query_parts.append(part_grad)
    query_rot_grad = jnp.concatenate(query_parts, axis=1).reshape(
        sequence_group, token_per_shard, QUERY_HEADS, HEAD_SIZE
    )
    query_grad_r = (
        rotary_inverse(query_rot_grad, cosine_table, sine_table)
        .reshape(sequence_group, token_per_shard, QUERY_HEADS * HEAD_SIZE)
        .astype(jnp.bfloat16)
    )
    key_backward, value_back = (
        lax.psum_scatter(
            key_accumulator.reshape(sequence_group, length_value, kv_width),
            "ctx",
            scatter_dimension=1,
            tiled=True,
        ),
        lax.psum_scatter(
            value_accumulator.reshape(sequence_group, length_value, kv_width),
            "ctx",
            scatter_dimension=1,
            tiled=True,
        ),
    )
    key_grad_r = (
        rotary_inverse(
            key_backward.reshape(sequence_group, token_per_shard, KEY_VALUE_HEADS, HEAD_SIZE),
            cosine_table,
            sine_table,
        )
        .reshape(sequence_group, token_per_shard, kv_width)
        .astype(jnp.bfloat16)
    )
    value_grad_r = value_back.astype(jnp.bfloat16)
    query_wgrad = outer_sum(hidden_one, query_grad_r)
    key_wgrad = outer_sum(hidden_one, key_grad_r)
    value_wgrad = outer_sum(hidden_one, value_grad_r)
    hidden_one_grad = (
        back_dot(query_grad_r, query_full)
        + back_dot(key_grad_r, key_full)
        + back_dot(value_grad_r, value_full)
    )
    attn_gain_wgrad = jnp.sum(hidden_one_grad * normed_one, axis=(0, 1))
    input_grad = mixed_grad + rms_back(hidden_one_grad * attn_gain_f, inv_one, normed_one)
    (
        query_part,
        key_portion,
        value_portion,
        output_part,
        attn_gain_part,
        mlp_gain_part,
        gate_part,
        up_part,
        down_part,
    ) = (
        lax.psum_scatter(
            query_wgrad.astype(jnp.bfloat16), "fsdp", scatter_dimension=0, tiled=True
        ).astype(jnp.float32),
        lax.psum_scatter(
            key_wgrad.astype(jnp.bfloat16), "fsdp", scatter_dimension=0, tiled=True
        ).astype(jnp.float32),
        lax.psum_scatter(
            value_wgrad.astype(jnp.bfloat16), "fsdp", scatter_dimension=0, tiled=True
        ).astype(jnp.float32),
        lax.psum_scatter(
            output_wgrad.astype(jnp.bfloat16), "fsdp", scatter_dimension=0, tiled=True
        ).astype(jnp.float32),
        lax.psum_scatter(
            attn_gain_wgrad.astype(jnp.bfloat16), "fsdp", scatter_dimension=0, tiled=True
        ).astype(jnp.float32),
        lax.psum_scatter(
            mlp_gain_wgrad.astype(jnp.bfloat16), "fsdp", scatter_dimension=0, tiled=True
        ).astype(jnp.float32),
        lax.psum_scatter(
            gate_wgrad.astype(jnp.bfloat16), "fsdp", scatter_dimension=1, tiled=True
        ).astype(jnp.float32),
        lax.psum_scatter(
            up_wgrad.astype(jnp.bfloat16), "fsdp", scatter_dimension=1, tiled=True
        ).astype(jnp.float32),
        lax.psum_scatter(
            down_wgrad.astype(jnp.bfloat16), "fsdp", scatter_dimension=0, tiled=True
        ).astype(jnp.float32),
    )
    (
        query_total,
        key_total,
        value_total,
        output_total,
        attn_gain_total,
        mlp_gain_total,
        gate_total,
        up_total,
        down_total,
    ) = lax.psum(
        (
            query_part,
            key_portion,
            value_portion,
            output_part,
            attn_gain_part,
            mlp_gain_part,
            gate_part,
            up_part,
            down_part,
        ),
        "ctx",
    )
    return (
        block_out,
        input_grad,
        query_total,
        key_total,
        value_total,
        output_total,
        attn_gain_total,
        mlp_gain_total,
        gate_total,
        up_total,
        down_total,
    )


def solution(mesh):
    return jax.shard_map(
        body,
        mesh=mesh,
        in_specs=(
            P("fsdp", "ctx", None),
            P("fsdp", None),
            P("fsdp", None),
            P("fsdp", None),
            P("fsdp", None),
            P("fsdp"),
            P("fsdp"),
            P(None, "fsdp"),
            P(None, "fsdp"),
            P("fsdp", None),
            P(),
            P("fsdp", None),
            P("fsdp", "ctx", None),
        ),
        out_specs=(
            P("fsdp", "ctx", None),
            P("fsdp", "ctx", None),
            P("fsdp", None),
            P("fsdp", None),
            P("fsdp", None),
            P("fsdp", None),
            P("fsdp"),
            P("fsdp"),
            P(None, "fsdp"),
            P(None, "fsdp"),
            P("fsdp", None),
        ),
        check_vma=False,
    )
```

profile of v0, /device:TPU:1, one launch (start us, length us, event | category | flops | bytes accessed | tf_op | source)
XLA Modules:
  0.0 673.3 jit_solution(12008839852724974834)
XLA Ops:
  22.2 10.1 %all_gather.34 = bf16[576,192]{1,0:T(8,128)(2,1)S(1)} all-gather(bf16[288,192]{1,0:T(8,128)(2,1)S(1)} %copy-done.56), channel_id=1, replica_groups=mesh['ctx'=16,'fsdp'=2] {'fsdp'}, dimensions={0}, use_global_device_ids=true | all-gather | bytes 331776 | tf_op jit(solution)/shard_map/all_gather | solution.py:261
  34.1 4.2 all-reduce.6
  40.0 26.6 %all_gather.35 = bf16[2,1024,192]{2,1,0:T(8,128)(2,1)S(1)} all-gather(bf16[2,64,192]{2,1,0:T(8,128)(2,1)S(1)} %add_convert_fusion.1), channel_id=1, replica_groups=mesh['ctx'=16,'fsdp'=2] {'ctx'}, dimensions={1}, use_global_device_ids=true | all-gather | bytes 835584 | tf_op jit(solution)/shard_map/all_gather | solution.py:295
  66.6 16.5 %all_gather.36 = bf16[576,576]{1,0:T(8,128)(2,1)S(1)} all-gather(bf16[288,576]{1,0:T(8,128)(2,1)S(1)} %copy-done.47), channel_id=1, replica_groups=mesh['ctx'=16,'fsdp'=2] {'fsdp'}, dimensions={0}, use_global_device_ids=true | all-gather | bytes 995328 | tf_op jit(solution)/shard_map/all_gather | solution.py:260
  85.0 5.5 all_gather.37
  90.7 24.7 %all_gather.38 = bf16[2,1024,192]{2,1,0:T(8,128)(2,1)} all-gather(bf16[2,64,192]{2,1,0:T(8,128)(2,1)S(1)} %convolution_convert_fusion.1), channel_id=1, replica_groups=mesh['ctx'=16,'fsdp'=2] {'ctx'}, dimensions={1}, use_global_device_ids=true | all-gather | bytes 835584 | tf_op jit(solution)/shard_map/all_gather | solution.py:296
  116.2 7.3 %while.65 = (s32[]{:T(128)}, f32[2,3,3,32]{3,2,1,0:T(4,128)S(1)}, f32[2,3,3,32]{3,2,1,0:T(4,128)S(1)}, f32[2,3,3,32,64]{4,3,2,1,0:T(8,128)}, s32[]{:T(128)}, /*i...) while((s32[]{:T(128)}, f32[2,3,3,32]{3,2,1,0:T(4,128)S(1)}, ...), condition=%wide.region_13.15_spmd, body=%wide.region_10.14_spmd.sunk | while | flops 39389640 | bytes 5809110 | solution.py:137
  127.5 7.3 %while.64 = (s32[]{:T(128)}, f32[2,3,3,32]{3,2,1,0:T(4,128)S(1)}, f32[2,3,3,32]{3,2,1,0:T(4,128)S(1)}, f32[2,3,3,32,64]{4,3,2,1,0:T(8,128)}, s32[]{:T(128)}, /*i...) while((s32[]{:T(128)}, f32[2,3,3,32]{3,2,1,0:T(4,128)S(1)}, ...), condition=%wide.region_7.9_spmd, body=%wide.region_4.8_spmd.sunk | while | flops 39389640 | bytes 5809110 | solution.py:137
  134.8 2.1 copy.238
  136.9 11.2 %all_gather.39 = bf16[576,576]{1,0:T(8,128)(2,1)S(1)} all-gather(bf16[288,576]{1,0:T(8,128)(2,1)} %param.27), channel_id=1, replica_groups=mesh['ctx'=16,'fsdp'=2] {'fsdp'}, dimensions={0}, use_global_device_ids=true | all-gather | bytes 995328 | tf_op jit(solution)/shard_map/all_gather | solution.py:263
  150.0 3.0 fusion.48
  153.0 2.8 fusion.54
  155.8 3.5 multiply_convert_fusion.1
  170.3 14.8 %while.66 = (s32[]{:T(128)}, f32[2,32,3,3,64]{4,1,3,2,0:T(8,128)}, f32[2,32,32,192]{3,2,1,0:T(8,128)}, f32[2,32,32,192]{3,2,1,0:T(8,128)}, s32[]{:T(128)}, /*ind...) while((s32[]{:T(128)}, f32[2,32,3,3,64]{4,1,3,2,0:T(8,128)}, ...), condition=%wide.region_20.22_spmd, body=%wide.region_17.21_spmd.sunk | while | flops 96011592 | bytes 16000950 | solution.py:214
  178.2 2.8 scatter_fusion
  182.3 2.7 scatter_fusion.1
  186.3 14.6 %while.67 = (s32[]{:T(128)}, f32[2,32,3,3,64]{4,1,3,2,0:T(8,128)S(1)}, f32[2,32,32,192]{3,2,1,0:T(8,128)}, f32[2,32,32,192]{3,2,1,0:T(8,128)}, s32[]{:T(128)}, /...) while((s32[]{:T(128)}, ...), condition=%wide.region_25.27_spmd, body=%wide.region_22.26_spmd.sunk | while | flops 96011592 | bytes 16495858 | solution.py:214
  194.2 2.7 scatter_fusion.2
  198.2 2.7 scatter_fusion.3
  206.3 71.8 %reduce-scatter.10.cloned.1.call-done = f32[2,64,192]{2,1,0:T(8,128)} async-done(((f32[2,1024,192]{2,1,0:T(8,128)}), f32[2,64,192]{2,1,0:T(8,128)}) %reduce-scatter.10.cloned.1.call-update) | async-done | bytes 98320 | tf_op jit(solution)/shard_map/reduce_scatter | solution.py:397
  280.6 62.2 %reduce-scatter.12.cloned.1.call-done = f32[2,64,192]{2,1,0:T(8,128)} async-done(((f32[2,1024,192]{2,1,0:T(8,128)}), f32[2,64,192]{2,1,0:T(8,128)}) %reduce-scatter.12.cloned.1.call-update) | async-done | bytes 98320 | tf_op jit(solution)/shard_map/reduce_scatter | solution.py:403
  351.4 2.1 fusion.73
  353.6 2.5 fusion.68
  356.1 6.9 %reduce-scatter.14.cloned.1.call-done = bf16[288,576]{1,0:T(8,128)(2,1)} async-done(((bf16[576,576]{1,0:T(8,128)(2,1)}), bf16[288,576]{1,0:T(8,128)(2,1)}) %reduce-scatter.14.cloned.1.call-update) | async-done | bytes 331792 | tf_op jit(solution)/shard_map/reduce_scatter | solution.py:441
  362.9 19.2 %reduce-scatter.20.cloned.1.call-done = bf16[288,576]{1,0:T(8,128)(2,1)} async-done(((bf16[576,576]{1,0:T(8,128)(2,1)}), bf16[288,576]{1,0:T(8,128)(2,1)}) %reduce-scatter.20.cloned.1.call-update) | async-done | bytes 331792 | tf_op jit(solution)/shard_map/reduce_scatter | solution.py:450
  383.7 3.8 all-reduce.5
  388.6 8.4 %reduce-scatter.16.cloned.1.call-done = bf16[288,192]{1,0:T(8,128)(2,1)} async-done(((bf16[576,192]{1,0:T(8,128)(2,1)}), bf16[288,192]{1,0:T(8,128)(2,1)}) %reduce-scatter.16.cloned.1.call-update) | async-done | bytes 110608 | tf_op jit(solution)/shard_map/reduce_scatter | solution.py:444
  397.0 14.3 %reduce-scatter.18.cloned.1.call-done = bf16[288,192]{1,0:T(8,128)(2,1)} async-done(((bf16[576,192]{1,0:T(8,128)(2,1)}), bf16[288,192]{1,0:T(8,128)(2,1)}) %reduce-scatter.18.cloned.1.call-update) | async-done | bytes 110608 | tf_op jit(solution)/shard_map/reduce_scatter | solution.py:447
  411.3 30.9 %reduce-scatter.22.cloned.1.call-done = bf16[576,768]{1,0:T(8,128)(2,1)} async-done(((bf16[576,1536]{1,0:T(8,128)(2,1)}), bf16[576,768]{1,0:T(8,128)(2,1)}) %reduce-scatter.22.cloned.1.call-update) | async-done | bytes 884752 | tf_op jit(solution)/shard_map/reduce_scatter | solution.py:459
  442.3 31.2 %reduce-scatter.24.cloned.1.call-done = bf16[576,768]{1,0:T(8,128)(2,1)} async-done(((bf16[576,1536]{1,0:T(8,128)(2,1)}), bf16[576,768]{1,0:T(8,128)(2,1)}) %reduce-scatter.24.cloned.1.call-update) | async-done | bytes 884752 | tf_op jit(solution)/shard_map/reduce_scatter | solution.py:462
  473.5 31.0 %reduce-scatter.26.cloned.1.call-done = bf16[768,576]{0,1:T(8,128)(2,1)} async-done(((bf16[1536,576]{0,1:T(8,128)(2,1)}), bf16[768,576]{0,1:T(8,128)(2,1)}) %reduce-scatter.26.cloned.1.call-update) | async-done | bytes 884752 | tf_op jit(solution)/shard_map/reduce_scatter | solution.py:465
  504.4 162.0 %all-reduce.8 = (f32[288,576]{1,0:T(8,128)}, f32[288,192]{1,0:T(8,128)}, f32[288,192]{1,0:T(8,128)}, f32[288,576]{1,0:T(8,128)}, f32[288]{0:T(512)}, /*index=5*/...) all-reduce(bf16[288,576]{1,0:T(8,128)(2,1)S(1)} %copy-done.48, ...), channel_id=1, replica_groups=mesh['ctx'=16,'fsdp'=2] {'ctx'}, use_global_device_ids=true, to_apply=%region_30.32 | all-reduce | flops 1770048 | bytes 10621440 | tf_op jit(solution)/shard_map/psum | solution.py:479
  (373 shorter events, 81.6 us)
Async XLA Ops:
  7.2 15.0 %copy-start.56 = (bf16[288,192]{1,0:T(8,128)(2,1)S(1)}, bf16[288,192]{1,0:T(8,128)(2,1)}, u32[]{:S(2)}) copy-start(bf16[288,192]{1,0:T(8,128)(2,1)} %param.25) | copy-start | bytes 331780
  7.2 142.8 %all-gather.8.cloned.1.call-start = ((), (), s32[]{:S(2)}) async-start(), calls=%async_computation.11 | async-start | bytes 2654208 | tf_op jit(solution)/shard_map/all_gather | solution.py:343
  7.9 24.4 %copy-start.73 = (u32[32]{0:T(128)S(1)}, u32[32]{0:T(128)}, u32[]{:S(2)}) copy-start(u32[32]{0:T(128)} %constant.390) | copy-start | bytes 388
  8.0 25.6 %copy-start.74 = (bf16[288]{0:T(512)(128)(2,1)S(1)}, bf16[288]{0:T(512)(128)(2,1)}, u32[]{:S(2)}) copy-start(bf16[288]{0:T(512)(128)(2,1)} %param.28) | copy-start | bytes 1732
  8.0 25.9 %copy-start.75 = (bf16[288]{0:T(512)(128)(2,1)S(1)}, bf16[288]{0:T(512)(128)(2,1)}, u32[]{:S(2)}) copy-start(bf16[288]{0:T(512)(128)(2,1)} %param.29) | copy-start | bytes 1732
  8.0 30.3 %copy-start.5 = (bf16[2,64,576]{2,1,0:T(8,128)(2,1)S(1)}, bf16[2,64,576]{2,1,0:T(8,128)(2,1)}, u32[]{:S(2)}) copy-start(bf16[2,64,576]{2,1,0:T(8,128)(2,1)} %param.23) | copy-start | bytes 442372
  8.0 145.0 %all-gather.6.cloned.1.call-start = ((), (), s32[]{:S(2)}) async-start(), calls=%async_computation.10 | async-start | bytes 2654208 | tf_op jit(solution)/shard_map/all_gather | solution.py:342
  8.7 147.1 %all-gather.4.cloned.1.call-start = ((), (), s32[]{:S(2)}) async-start(), calls=%async_computation.9 | async-start | bytes 2654208 | tf_op jit(solution)/shard_map/all_gather | solution.py:341
  9.5 268.6 %reduce-scatter.10.cloned.1.call-start = ((), (), s32[]{:S(2)}) async-start(), calls=%async_computation.12 | async-start | bytes 2228224 | tf_op jit(solution)/shard_map/reduce_scatter | solution.py:397
  38.3 52.1 %copy-start.54 = (f32[576]{0:T(1024)}, f32[576]{0:T(1024)S(1)}, u32[]{:S(2)}) copy-start(f32[576]{0:T(1024)S(1)} %convert_element_type.172) | copy-start | bytes 6916
  38.4 52.0 %copy-start.66 = (f32[2,64]{1,0:T(2,128)}, f32[2,64]{1,0:T(2,128)S(1)}, u32[]{:S(2)}) copy-start(f32[2,64]{1,0:T(2,128)S(1)} %add_rsqrt_fusion.1) | copy-start | bytes 1540
  38.8 27.8 %copy-start.47 = (bf16[288,576]{1,0:T(8,128)(2,1)S(1)}, bf16[288,576]{1,0:T(8,128)(2,1)}, u32[]{:S(2)}) copy-start(bf16[288,576]{1,0:T(8,128)(2,1)} %param.24) | copy-start | bytes 995332
  39.2 44.5 %copy-start.38 = (f32[64,64]{0,1:T(8,128)}, f32[64,64]{0,1:T(8,128)S(1)}, u32[]{:S(2)}) copy-start(f32[64,64]{0,1:T(8,128)S(1)} %get-tuple-element.1172) | copy-start | bytes 49156
  90.4 25.7 %copy-start.34 = (bf16[576,192]{1,0:T(8,128)(2,1)}, bf16[576,192]{1,0:T(8,128)(2,1)S(1)}, u32[]{:S(2)}) copy-start(bf16[576,192]{1,0:T(8,128)(2,1)S(1)} %all_gather.37) | copy-start | bytes 663556
  134.8 13.3 %copy-start.14 = (f32[2,3,3,32,64]{3,4,2,1,0:T(8,128)S(1)}, f32[2,3,3,32,64]{3,4,2,1,0:T(8,128)}, u32[]{:S(2)}) copy-start(f32[2,3,3,32,64]{3,4,2,1,0:T(8,128)} %copy.241) | copy-start | bytes 442372
  201.0 141.8 %reduce-scatter.12.cloned.1.call-start = ((), (), s32[]{:S(2)}) async-start(), calls=%async_computation.13 | async-start | bytes 2228224 | tf_op jit(solution)/shard_map/reduce_scatter | solution.py:403
  201.5 161.4 %reduce-scatter.14.cloned.1.call-start = ((), (), s32[]{:S(2)}) async-start(), calls=%async_computation.14 | async-start | bytes 1105920 | tf_op jit(solution)/shard_map/reduce_scatter | solution.py:441
  204.8 74.6 %copy-start.36 = (f32[64,192]{1,0:T(8,128)S(1)}, f32[64,192]{1,0:T(8,128)}, u32[]{:S(2)}) copy-start(f32[64,192]{1,0:T(8,128)} %copy-done.35) | copy-start | bytes 147460
  204.8 177.3 %reduce-scatter.20.cloned.1.call-start = ((), (), s32[]{:S(2)}) async-start(), calls=%async_computation.17 | async-start | bytes 1105920 | tf_op jit(solution)/shard_map/reduce_scatter | solution.py:450
  206.2 190.8 %reduce-scatter.16.cloned.1.call-start = ((), (), s32[]{:S(2)}) async-start(), calls=%async_computation.15 | async-start | bytes 442368 | tf_op jit(solution)/shard_map/reduce_scatter | solution.py:444
  279.2 65.6 %copy-start.24 = (bf16[2,64,576]{2,1,0:T(8,128)(2,1)S(1)}, bf16[2,64,576]{2,1,0:T(8,128)(2,1)}, u32[]{:S(2)}) copy-start(bf16[2,64,576]{2,1,0:T(8,128)(2,1)} %copy-done.23) | copy-start | bytes 442372
  279.2 65.6 %copy-start.29 = (bf16[2,64,1536]{2,1,0:T(8,128)(2,1)S(1)}, bf16[2,64,1536]{2,1,0:T(8,128)(2,1)}, u32[]{:S(2)}) copy-start(bf16[2,64,1536]{2,1,0:T(8,128)(2,1)} %copy-done.28) | copy-start | bytes 1179652
  280.5 130.8 %reduce-scatter.18.cloned.1.call-start = ((), (), s32[]{:S(2)}) async-start(), calls=%async_computation.16 | async-start | bytes 442368 | tf_op jit(solution)/shard_map/reduce_scatter | solution.py:447
  344.8 97.5 %reduce-scatter.22.cloned.1.call-start = ((), (), s32[]{:S(2)}) async-start(), calls=%async_computation.18 | async-start | bytes 2654208 | tf_op jit(solution)/shard_map/reduce_scatter | solution.py:459
  346.7 126.7 %reduce-scatter.24.cloned.1.call-start = ((), (), s32[]{:S(2)}) async-start(), calls=%async_computation.19 | async-start | bytes 2654208 | tf_op jit(solution)/shard_map/reduce_scatter | solution.py:462
  348.7 155.7 %reduce-scatter.26.cloned.1.call-start = ((), (), s32[]{:S(2)}) async-start(), calls=%async_computation.20 | async-start | bytes 2654208 | tf_op jit(solution)/shard_map/reduce_scatter | solution.py:465
  353.6 28.6 %copy-start.19 = (bf16[576,192]{1,0:T(8,128)(2,1)S(1)}, bf16[576,192]{1,0:T(8,128)(2,1)}, u32[]{:S(2)}) copy-start(bf16[576,192]{1,0:T(8,128)(2,1)} %copy-done.18) | copy-start | bytes 663556
  353.6 28.6 %copy-start.33 = (f32[2,64,576]{2,1,0:T(8,128)S(1)}, f32[2,64,576]{2,1,0:T(8,128)}, u32[]{:S(2)}) copy-start(f32[2,64,576]{2,1,0:T(8,128)} %fusion.73) | copy-start | bytes 884740
  353.6 28.8 %copy-start.40 = (f32[2,64,192]{2,1,0:T(8,128)S(1)}, f32[2,64,192]{2,1,0:T(8,128)}, u32[]{:S(2)}) copy-start(f32[2,64,192]{2,1,0:T(8,128)} %reduce-scatter.12.cloned.1.call-done) | copy-start | bytes 294916
  356.1 27.7 %copy-start.71 = (bf16[576]{0:T(1024)(128)(2,1)S(1)}, bf16[576]{0:T(1024)(128)(2,1)}, u32[]{:S(2)}) copy-start(bf16[576]{0:T(1024)(128)(2,1)} %get-tuple-element.986) | copy-start | bytes 3460
  362.9 141.5 %copy-start.48 = (bf16[288,576]{1,0:T(8,128)(2,1)S(1)}, bf16[288,576]{1,0:T(8,128)(2,1)}, u32[]{:S(2)}) copy-start(bf16[288,576]{1,0:T(8,128)(2,1)} %reduce-scatter.14.cloned.1.call-done) | copy-start | bytes 995332
  382.1 122.3 %copy-start.49 = (bf16[288,576]{1,0:T(8,128)(2,1)S(1)}, bf16[288,576]{1,0:T(8,128)(2,1)}, u32[]{:S(2)}) copy-start(bf16[288,576]{1,0:T(8,128)(2,1)} %reduce-scatter.20.cloned.1.call-done) | copy-start | bytes 995332
  (56 other events, 176.1 us)
Sparse Core Ops, SparseCore 0:
  9.6 34.7 all-gather.7
  45.9 34.4 all-gather.5
  81.9 32.3 all-gather.3
  201.1 76.9 reduce-scatter.9
  282.1 60.5 reduce-scatter.11
  345.5 17.4 reduce-scatter.13
  365.2 16.8 reduce-scatter.19
  384.9 12.0 reduce-scatter.15
  399.2 12.0 reduce-scatter.17
  414.0 28.2 reduce-scatter.21
  445.2 28.2 reduce-scatter.23
  476.2 28.2 reduce-scatter.25
where the time goes:
time: 676 us; the launch traced here: 673 us
  waiting for transfers between devices  279 us (41%)
  blocking collectives  265 us (39%)
  local copies, waits for them, and re-layouts  44.2 us (7%)
  matrix products  39.3 us (6%)
  between operations  23.1 us (3%)
  other arithmetic  21.8 us (3%)
    psum x1, blocking collectives, body(): lax.psum((query_part, key_portion, value_portion, output_part, attn_gain_...  162 us
    reduce_scatter x1, waiting for transfers between devices, body(): lax.psum_scatter(key_accumulator.reshape(sequence_group, length_value, kv...  71.8 us
    reduce_scatter x1, waiting for transfers between devices, body(): lax.psum_scatter(value_accumulator.reshape(sequence_group, length_value,...  62.2 us
    reduce_scatter x1, waiting for transfers between devices, body(): lax.psum_scatter(up_wgrad.astype(jnp.bfloat16), 'fsdp', scatter_dimension...  31.2 us
    reduce_scatter x1, waiting for transfers between devices, body(): lax.psum_scatter(down_wgrad.astype(jnp.bfloat16), 'fsdp', scatter_dimensi...  31 us
    reduce_scatter x1, waiting for transfers between devices, body(): lax.psum_scatter(gate_wgrad.astype(jnp.bfloat16), 'fsdp', scatter_dimensi...  30.9 us
    all_gather x1, blocking collectives, body(): lax.all_gather(key_rows, 'ctx', axis=1, tiled=True)  26.6 us
    all_gather x1, blocking collectives, body(): lax.all_gather(value_rows, 'ctx', axis=1, tiled=True)  24.7 us
  transfers between devices with their start and end apart: 12, of which 9 were waited for; matrix products, arithmetic and copies ran while one was open for 9% of the time, Pallas kernels for 0%

commit v1 on v0

v1 whole, which is shorter than its diff:
```python
import functools
import math

import jax
import jax.numpy as jnp
from jax import lax
from jax.experimental import pallas as pl
from jax.experimental.pallas import tpu as pltpu
from jax.sharding import PartitionSpec as P

QUERY_HEADS = 9
KEY_VALUE_HEADS = 3
HEAD_SIZE = 64
GROUP = QUERY_HEADS // KEY_VALUE_HEADS
KV_WIDTH = KEY_VALUE_HEADS * HEAD_SIZE
SCALE = 1.0 / math.sqrt(HEAD_SIZE)

epsilon = 1e-05
theta_base = 10000.0
masked_logits = -1e30

VMEM = pl.BlockSpec(memory_space=pltpu.VMEM)
SMEM = pl.BlockSpec(memory_space=pltpu.SMEM)
MESH = pl.DeviceIdType.MESH
F32 = jnp.float32
BF16 = jnp.bfloat16


class Place:
    def __init__(self, members):
        self.members = members
        self.ctx = lax.axis_index("ctx")
        self.fsdp = lax.axis_index("fsdp")
        self.core = self.ctx % 2
        self.x = (self.ctx // 2) % 2
        self.far = self.ctx // 4

    def own(self, axis):
        return {"core": self.core, "x": self.x, "y": self.fsdp}[axis]

    def partner(self, axis):
        if axis == "core":
            return (self.ctx + 1 - 2 * self.core, self.fsdp)
        if axis == "x":
            return (self.ctx + 2 - 4 * self.x, self.fsdp)
        return (self.ctx, 1 - self.fsdp)

    def far_member(self, step):
        return (self.far + step) % self.members

    def far_device(self, step):
        return (self.far_member(step) * 4 + self.ctx % 4, self.fsdp)

    def greet(self, axes, far):
        barrier = pltpu.get_barrier_semaphore()
        for axis in axes:
            pl.semaphore_signal(barrier, inc=1, device_id=self.partner(axis), device_id_type=MESH)
        count = len(axes)
        if far:
            for step in range(1, self.members):
                pl.semaphore_signal(
                    barrier, inc=1, device_id=self.far_device(step), device_id_type=MESH
                )
            count += self.members - 1
        pl.semaphore_wait(barrier, count)


class Sems:
    def __init__(self, send, recv):
        self.send, self.recv, self.at = send, recv, 0

    def copy(self, src, dst, device):
        at = self.at
        self.at += 1
        made = pltpu.make_async_remote_copy(
            src_ref=src,
            dst_ref=dst,
            send_sem=self.send.at[at],
            recv_sem=self.recv.at[at],
            device_id=device,
            device_id_type=MESH,
        )
        made.start()
        return made


def params(collective_id):
    return pltpu.CompilerParams(
        collective_id=collective_id, has_side_effects=True, vmem_limit_bytes=60 * 2**20
    )


def weights_kernel(members, count, *refs):
    ins, gain_in = refs[:count], refs[count]
    outs, gain_out = refs[count + 1 : 2 * count + 1], refs[2 * count + 1]
    send, recv = refs[2 * count + 2 :]
    me = Place(members)
    me.greet(("core", "y"), False)
    sems = Sems(send, recv)
    rows = ins[0].shape[0]
    half = rows // 2
    first = []
    for src, dst in zip(ins, outs):
        take = pl.ds(pl.multiple_of(me.core * half, 16), half)
        put = pl.ds(pl.multiple_of(me.fsdp * rows + me.core * half, 16), half)
        first.append(sems.copy(src.at[take], dst.at[put], me.partner("y")))
    gain = sems.copy(gain_in, gain_out.at[me.fsdp], me.partner("y"))
    gain_out[me.fsdp] = gain_in[...]
    for src, dst in zip(ins, outs):
        dst[pl.ds(pl.multiple_of(me.fsdp * rows, 16), rows)] = src[...]
    second = []
    for copy, dst in zip(first, outs):
        copy.wait_recv()
        put = pl.ds(pl.multiple_of((1 - me.fsdp) * rows + me.core * half, 16), half)
        second.append(sems.copy(dst.at[put], dst.at[put], me.partner("core")))
    for copy in second:
        copy.wait()
    for copy in first:
        copy.wait_send()
    gain.wait()


def gather_weights(members, weights, gains):
    count = len(weights)
    return pl.pallas_call(
        functools.partial(weights_kernel, members, count),
        out_shape=[jax.ShapeDtypeStruct((2 * w.shape[0], w.shape[1]), w.dtype) for w in weights]
        + [jax.ShapeDtypeStruct((2,) + gains.shape, gains.dtype)],
        in_specs=[VMEM] * (count + 1),
        out_specs=[VMEM] * (count + 1),
        scratch_shapes=[pltpu.SemaphoreType.DMA((2 * count + 1,))] * 2,
        compiler_params=params(0),
    )(*weights, gains)


def keys_kernel(members, kv_ref, grad_ref, out_ref, other_ref, send, recv):
    me = Place(members)
    me.greet(("core", "x", "y"), True)
    sems = Sems(send, recv)
    mine = out_ref.at[me.core, me.x, me.far]
    far = [sems.copy(kv_ref, mine, me.far_device(step)) for step in range(1, members)]
    own = sems.copy(kv_ref, mine, me.partner("x"))
    swap = sems.copy(grad_ref, other_ref, me.partner("y"))
    out_ref[me.core, me.x, me.far] = kv_ref[...]
    along = []
    for step in range(1, members):
        far[step - 1].wait_recv()
        got = out_ref.at[me.core, me.x, me.far_member(members - step)]
        along.append(sems.copy(got, got, me.partner("x")))
    own.wait_recv()
    for copy in along:
        copy.wait_recv()
    block = out_ref.at[me.core]
    last = sems.copy(block, block, me.partner("core"))
    last.wait()
    swap.wait()
    own.wait_send()
    for copy in far + along:
        copy.wait_send()


def gather_keys(members, kv, grad):
    count = 2 * (members - 1) + 3
    return pl.pallas_call(
        functools.partial(keys_kernel, members),
        out_shape=[
            jax.ShapeDtypeStruct((2, 2, members) + kv.shape, kv.dtype),
            jax.ShapeDtypeStruct(grad.shape, grad.dtype),
        ],
        in_specs=[VMEM] * 2,
        out_specs=[VMEM] * 2,
        scratch_shapes=[pltpu.SemaphoreType.DMA((count,))] * 2,
        compiler_params=params(1),
    )(kv, grad)


def swap_kernel(members, count, *refs):
    ins, outs = refs[:count], refs[count : 2 * count]
    send, recv = refs[2 * count :]
    me = Place(members)
    me.greet(("y",), False)
    sems = Sems(send, recv)
    copies = [sems.copy(src, dst, me.partner("y")) for src, dst in zip(ins, outs)]
    for copy in copies:
        copy.wait()


def swap_rows(members, collective_id, *arrays):
    count = len(arrays)
    return pl.pallas_call(
        functools.partial(swap_kernel, members, count),
        out_shape=[jax.ShapeDtypeStruct(a.shape, a.dtype) for a in arrays],
        in_specs=[VMEM] * count,
        out_specs=[VMEM] * count,
        scratch_shapes=[pltpu.SemaphoreType.DMA((count,))] * 2,
        compiler_params=params(collective_id),
    )(*arrays)


def add(a, b):
    return (a.astype(F32) + b.astype(F32)).astype(BF16)


def reduce_kernel(members, flows, has_small, *refs):
    refs = list(refs)
    ins = [refs.pop(0) for _ in flows]
    small_in = refs.pop(0) if has_small else None
    outs = [refs.pop(0) for _ in flows]
    small_out = refs.pop(0) if has_small else None
    gots = [[refs.pop(0) for _ in axes] for axes, _ in flows]
    far_gots = [refs.pop(0) for _ in flows]
    axes_all = []
    for axes, _ in flows:
        axes_all += [axis for axis in axes if axis not in axes_all]
    if has_small:
        small_acc = refs.pop(0)
        small_got = refs.pop(0)
        small_far = refs.pop(0)
    send, recv = refs
    me = Place(members)
    me.greet(tuple(axes_all), True)
    sems = Sems(send, recv)
    sent = []

    def go(src, dst, device):
        copy = sems.copy(src, dst, device)
        sent.append(copy)
        return copy

    flying = []
    for f, (axes, _) in enumerate(flows):
        flying.append(
            go(ins[f].at[1 - me.own(axes[0])], gots[f][0], me.partner(axes[0]))
        )
    depth = max(len(axes) for axes, _ in flows)
    far_flying = [None] * len(flows)
    small = None
    if has_small:
        small_acc[0] = small_in[...]
        small = go(small_acc.at[0], small_got.at[0], me.partner(axes_all[0]))
    for level in range(depth):
        for f, (axes, _) in enumerate(flows):
            if level >= len(axes):
                continue
            flying[f].wait_recv()
            source = ins[f] if level == 0 else gots[f][level - 1]
            held = source.at[me.own(axes[level])]
            got = total = gots[f][level]
            if level + 1 < len(axes):
                away = 1 - me.own(axes[level + 1])
                keep = me.own(axes[level + 1])
                total[away] = add(held[away], got[away])
                flying[f] = go(
                    total.at[away], gots[f][level + 1], me.partner(axes[level + 1])
                )
                total[keep] = add(held[keep], got[keep])
            else:
                far_flying[f] = []
                for step in range(1, members):
                    to = me.far_member(step)
                    total[to] = add(held[to], got[to])
                    far_flying[f].append(
                        go(total.at[to], far_gots[f].at[step - 1], me.far_device(step))
                    )
                total[me.far] = add(held[me.far], got[me.far])
        if has_small:
            small.wait_recv()
            small_acc[level + 1] = small_acc[level] + small_got[level]
            if level + 1 < depth:
                small = go(
                    small_acc.at[level + 1],
                    small_got.at[level + 1],
                    me.partner(axes_all[level + 1]),
                )
            else:
                small = [
                    go(small_acc.at[level + 1], small_far.at[step - 1], me.far_device(step))
                    for step in range(1, members)
                ]
    back = [None] * len(flows)
    for f, (axes, gather) in enumerate(flows):
        whole = gots[f][-1][me.far].astype(F32)
        for step in range(1, members):
            far_flying[f][step - 1].wait_recv()
            whole = whole + far_gots[f][step - 1].astype(F32)
        if not gather:
            outs[f][...] = whole
            continue
        outs[f][me.core, me.x, me.far] = whole.astype(BF16)
        mine = outs[f].at[me.core, me.x, me.far]
        back[f] = [go(mine, mine, me.far_device(step)) for step in range(1, members)]
    if has_small:
        whole = small_acc[depth]
        for step in range(1, members):
            small[step - 1].wait_recv()
            whole = whole + small_far[step - 1]
        small_out[...] = whole
    for axis in ("x", "core"):
        for f, (axes, gather) in enumerate(flows):
            if gather:
                for copy in back[f]:
                    copy.wait_recv()
                block = outs[f].at[me.core, me.x] if axis == "x" else outs[f].at[me.core]
                back[f] = [go(block, block, me.partner(axis))]
    for f, (axes, gather) in enumerate(flows):
        if gather:
            back[f][0].wait_recv()
    for copy in sent:
        copy.wait_send()


def reduce_chunks(members, collective_id, flows, arrays, small=None):
    flows = tuple((tuple(axes), gather) for axes, gather in flows)
    outs, gots, fars, count = [], [], [], 0
    for (axes, gather), array in zip(flows, arrays):
        chunk = array.shape[len(axes) + 1 :]
        if gather:
            outs.append(jax.ShapeDtypeStruct((2, 2, members) + chunk, array.dtype))
        else:
            outs.append(jax.ShapeDtypeStruct(chunk, F32))
        for level in range(len(axes)):
            gots.append(pltpu.VMEM(array.shape[level + 1 :], array.dtype))
        fars.append(pltpu.VMEM((members - 1,) + chunk, array.dtype))
        count += len(axes) + members - 1 + (members + 1 if gather else 0)
    depth = max(len(axes) for axes, _ in flows)
    scratch = gots + fars
    operands = list(arrays)
    if small is not None:
        outs.append(jax.ShapeDtypeStruct(small.shape, small.dtype))
        scratch += [
            pltpu.VMEM((depth + 1,) + small.shape, small.dtype),
            pltpu.VMEM((depth,) + small.shape, small.dtype),
            pltpu.VMEM((members - 1,) + small.shape, small.dtype),
        ]
        operands.append(small)
        count += depth + members - 1
    return pl.pallas_call(
        functools.partial(reduce_kernel, members, flows, small is not None),
        out_shape=outs,
        in_specs=[VMEM] * len(operands),
        out_specs=[VMEM] * len(outs),
        scratch_shapes=scratch + [pltpu.SemaphoreType.DMA((count,))] * 2,
        compiler_params=params(collective_id),
    )(*operands)


def lane_mask(base, head):
    lane = lax.broadcasted_iota(jnp.int32, (1, 2 * KV_WIDTH), 1)
    low = base + head * HEAD_SIZE
    return jnp.where((lane >= low) & (lane < low + HEAD_SIZE), 1.0, 0.0).astype(F32)


def spread(ref, part, base):
    rows = []
    for group in range(GROUP):
        value = ref[part, group].astype(F32)
        for head in range(KEY_VALUE_HEADS):
            rows.append(value * lane_mask(base, head))
    return jnp.concatenate(rows, axis=0)


def fold(value, base, out_ref, part, block):
    for group in range(GROUP):
        total = None
        for head in range(KEY_VALUE_HEADS):
            low = (group * KEY_VALUE_HEADS + head) * block
            piece = value[low : low + block] * lane_mask(base, head)
            total = piece if total is None else total + piece
        out_ref[part, group] = total


def key_window(kv_ref, slot_ref, half, seq, window):
    return jnp.concatenate(
        [
            kv_ref[slot_ref[half * window + j], seq * 2 + slot_ref[(2 + half) * window + j]]
            for j in range(window)
        ],
        axis=0,
    )


def nt(a, b):
    return lax.dot_general(a, b, (((1,), (1,)), ((), ())), preferred_element_type=F32)


def tn(a, b):
    return lax.dot_general(a, b, (((0,), (0,)), ((), ())), preferred_element_type=F32)


def attend_kernel(window, block, slot_ref, q_ref, kv_ref, bias_ref, out_ref, lse_ref):
    for seq in range(2):
        for half in range(2):
            part = seq * 2 + half
            keys = key_window(kv_ref, slot_ref, half, seq, window)
            query = spread(q_ref, part, 0).astype(BF16)
            bias = jnp.concatenate([bias_ref[part]] * QUERY_HEADS, axis=0)
            scores = nt(query, keys) * SCALE + bias
            top = jnp.max(scores, axis=-1, keepdims=True)
            weights = jnp.exp(scores - top)
            total = jnp.sum(weights, axis=-1, keepdims=True)
            probs = (weights / total).astype(BF16)
            mixed = jnp.dot(probs, keys, preferred_element_type=F32)
            fold(mixed, KV_WIDTH, out_ref, part, block)
            lse_ref[part] = top + jnp.log(total)


def attend(slots, query, kv, bias, window, block):
    return pl.pallas_call(
        functools.partial(attend_kernel, window, block),
        out_shape=[
            jax.ShapeDtypeStruct(query.shape, F32),
            jax.ShapeDtypeStruct((4, QUERY_HEADS * block, 1), F32),
        ],
        in_specs=[SMEM] + [VMEM] * 3,
        out_specs=[VMEM] * 2,
        compiler_params=pltpu.CompilerParams(vmem_limit_bytes=60 * 2**20),
    )(slots, query, kv, bias)


def attend_back_kernel(
    window, block, slot_ref, q_ref, kv_ref, bias_ref, grad_ref, o_ref, lse_ref, dq_ref, dkv_ref
):
    dkv_ref[...] = jnp.zeros_like(dkv_ref)
    for seq in range(2):
        for half in range(2):
            part = seq * 2 + half
            keys = key_window(kv_ref, slot_ref, half, seq, window)
            query = spread(q_ref, part, 0).astype(BF16)
            bias = jnp.concatenate([bias_ref[part]] * QUERY_HEADS, axis=0)
            probs = jnp.exp(nt(query, keys) * SCALE + bias - lse_ref[part])
            grad32 = spread(grad_ref, part, KV_WIDTH)
            mixed = spread(o_ref, part, KV_WIDTH)
            delta = jnp.sum(grad32 * mixed, axis=-1, keepdims=True)
            grad = grad32.astype(BF16)
            score_grad = (probs * (nt(grad, keys) - delta)).astype(BF16)
            fold(
                jnp.dot(score_grad, keys, preferred_element_type=F32) * SCALE,
                0,
                dq_ref,
                part,
                block,
            )
            back = tn(score_grad, query) * SCALE + tn(probs.astype(BF16), grad)
            for j in range(window):
                at = slot_ref[half * window + j]
                row = seq * 2 + slot_ref[(2 + half) * window + j]
                dkv_ref[at, row] = add(dkv_ref[at, row], back[j * block : (j + 1) * block])


def attend_back(slots, query, kv, bias, grad, mixed, lse, window, block):
    return pl.pallas_call(
        functools.partial(attend_back_kernel, window, block),
        out_shape=[
            jax.ShapeDtypeStruct(query.shape, F32),
            jax.ShapeDtypeStruct(kv.shape, kv.dtype),
        ],
        in_specs=[SMEM] + [VMEM] * 6,
        out_specs=[VMEM] * 2,
        compiler_params=pltpu.CompilerParams(vmem_limit_bytes=60 * 2**20),
    )(slots, query, kv, bias, grad, mixed, lse)


def rope_tables(token_positions):
    half = HEAD_SIZE // 2
    freq = theta_base ** (-jnp.arange(half, dtype=jnp.float32) * 2.0 / HEAD_SIZE)
    angles = token_positions.astype(jnp.float32)[:, None] * freq[None, :]
    cosine_table = jnp.concatenate([jnp.cos(angles), jnp.cos(angles)], axis=-1)
    sine_table = jnp.concatenate([jnp.sin(angles), jnp.sin(angles)], axis=-1)
    return (cosine_table[:, None, :], sine_table[:, None, :])


def rotary_apply(value_rows, cosine_table, sine_table):
    half = value_rows.shape[-1] // 2
    turned = jnp.concatenate([-value_rows[..., half:], value_rows[..., :half]], axis=-1)
    return value_rows * cosine_table + turned * sine_table


def rotary_inverse(grads, cosine_table, sine_table):
    half = grads.shape[-1] // 2
    scaled = grads * sine_table
    turned = jnp.concatenate([scaled[..., half:], -scaled[..., :half]], axis=-1)
    return grads * cosine_table + turned


def normalize(value_rows):
    inverse = lax.rsqrt(jnp.mean(value_rows * value_rows, axis=-1, keepdims=True) + epsilon)
    return (inverse, value_rows * inverse)


def rms_back(grads, inverse, normed):
    return inverse * (grads - normed * jnp.mean(grads * normed, axis=-1, keepdims=True))


def outer_sum(left, right):
    flat_left = left.reshape(-1, left.shape[-1])
    flat_right = right.reshape(-1, right.shape[-1])
    return lax.dot_general(
        flat_left, flat_right, (((0,), (0,)), ((), ())), preferred_element_type=jnp.float32
    )


def back_dot(grads, weight):
    return lax.dot_general(
        grads, weight, (((grads.ndim - 1,), (1,)), ((), ())), preferred_element_type=jnp.float32
    )


def to_groups(rows, block):
    split = rows.reshape(-1, block, KEY_VALUE_HEADS, GROUP, HEAD_SIZE)
    return jnp.transpose(split, (0, 3, 1, 2, 4)).reshape(-1, GROUP, block, KV_WIDTH)


def from_groups(parts, block):
    split = parts.reshape(-1, GROUP, block, KEY_VALUE_HEADS, HEAD_SIZE)
    return jnp.transpose(split, (0, 2, 3, 1, 4)).reshape(2, 2 * block, QUERY_HEADS * HEAD_SIZE)


def chunks(rows, members):
    count = 4 * members
    each = -(-rows.shape[0] // (count * 16)) * 16
    padded = jnp.pad(rows, ((0, count * each - rows.shape[0]), (0, 0)))
    return padded.reshape(2, 2, members, each, rows.shape[1])


def unchunk(array, rows):
    return array.reshape(-1, array.shape[-1])[:rows]


def body(
    tokens,
    query_matrix,
    key_projection,
    value_projection,
    output_matrix,
    attn_gain,
    mlp_gain,
    gate_matrix,
    up_matrix,
    down_matrix,
    pair_table,
    doc_ids,
    out_grad,
):
    sequence_group, token_per_shard, width = tokens.shape
    pairs = lax.axis_size("ctx")
    members = pairs // 4
    block = token_per_shard // 2
    length = token_per_shard * pairs
    blocks = 2 * pairs
    window = length // 8 // block + 1
    rows = sequence_group * token_per_shard
    me_f = lax.axis_index("fsdp")

    gains = jnp.pad(
        jnp.stack([attn_gain, mlp_gain]).astype(F32), ((0, 6), (0, 0))
    )
    query_full, key_full, value_full, output_full, gains_full = gather_weights(
        members, (query_matrix, key_projection, value_projection, output_matrix), gains
    )
    attn_gain_f = gains_full[:, 0].reshape(width)
    mlp_gain_f = gains_full[:, 1].reshape(width)

    table_row = lax.dynamic_index_in_dim(pair_table, lax.axis_index("ctx"), 0, keepdims=False)
    local = jnp.arange(token_per_shard, dtype=jnp.int32)
    own_pos = jnp.where(local < block, table_row[0], table_row[1]) * block + local % block
    cosine_table, sine_table = rope_tables(own_pos)

    block_ids = jnp.arange(blocks, dtype=jnp.int32)
    where_dealt = jnp.sum(
        block_ids[None, :]
        * (pair_table.reshape(-1)[None, :] == block_ids[:, None]).astype(jnp.int32),
        axis=1,
    )
    span = window * block
    padded_docs = jnp.pad(doc_ids, ((0, 0), (span - block, 0)), constant_values=-1)
    padded_slots = jnp.pad(where_dealt, (window - 1, 0))
    slot_parts, bias_parts = [], []
    offset = jnp.arange(span, dtype=jnp.int32)
    for half in range(2):
        at = table_row[half]
        slot_parts.append(lax.dynamic_slice_in_dim(padded_slots, at, window, 0))
        key_doc = lax.dynamic_slice_in_dim(padded_docs, at * block, span, 1)
        query_doc = key_doc[:, span - block :]
        causal = offset[None, :] <= offset[:block, None] + (span - block)
        allowed = causal[None] & (key_doc[:, None, :] == query_doc[:, :, None])
        bias_parts.append(jnp.where(allowed, 0.0, masked_logits))
    slots = jnp.concatenate(slot_parts)
    owner, which = slots // 2, slots % 2
    lies = (owner % 2) * (2 * members) + (owner // 2 % 2) * members + owner // 4
    slots = jnp.concatenate([lies, which]).astype(jnp.int32)
    bias = jnp.stack(bias_parts, axis=1).reshape(2 * sequence_group, block, span).astype(F32)

    inputs = tokens.astype(F32)
    inv_one, normed_one = normalize(inputs)
    hidden_one = (normed_one * attn_gain_f).astype(BF16)
    query_lin = jnp.dot(hidden_one, query_full, preferred_element_type=F32).reshape(
        sequence_group, token_per_shard, QUERY_HEADS, HEAD_SIZE
    )
    key_linear = jnp.dot(hidden_one, key_full, preferred_element_type=F32).reshape(
        sequence_group, token_per_shard, KEY_VALUE_HEADS, HEAD_SIZE
    )
    value_rows = jnp.dot(hidden_one, value_full, preferred_element_type=F32).astype(BF16)
    query_rows = rotary_apply(query_lin, cosine_table, sine_table).astype(BF16)
    key_rows = (
        rotary_apply(key_linear, cosine_table, sine_table)
        .astype(BF16)
        .reshape(sequence_group, token_per_shard, KV_WIDTH)
    )
    own_kv = jnp.concatenate([key_rows, value_rows], axis=-1).reshape(
        2 * sequence_group, block, 2 * KV_WIDTH
    )
    flat_grad = out_grad.reshape(rows, width)
    kv_all, other_grad = gather_keys(members, own_kv, flat_grad)
    kv_all = kv_all.reshape(pairs, 2 * sequence_group, block, 2 * KV_WIDTH)

    query_parts = jnp.pad(to_groups(query_rows, block), ((0, 0), (0, 0), (0, 0), (0, KV_WIDTH)))
    mixed_parts, lse = attend(slots, query_parts, kv_all, bias, window, block)
    attn_in = from_groups(mixed_parts[..., KV_WIDTH:].astype(BF16), block)

    mixed_heads = inputs + jnp.dot(attn_in, output_full, preferred_element_type=F32)
    inv_two, normed_two = normalize(mixed_heads)
    hidden_two = (normed_two * mlp_gain_f).astype(BF16).reshape(rows, width)

    (other_hidden,) = swap_rows(members, 2, hidden_two)
    hid = jnp.concatenate([hidden_two, other_hidden])
    grads = jnp.concatenate([flat_grad, other_grad])
    gate = jnp.dot(hid, gate_matrix, preferred_element_type=F32)
    upper = jnp.dot(hid, up_matrix, preferred_element_type=F32)
    sigma = jax.nn.sigmoid(gate)
    activated = (gate * sigma * upper).astype(BF16)
    act_grad = back_dot(grads, down_matrix)
    up_grad_r = (act_grad * gate * sigma).astype(BF16)
    gate_grad_r = (act_grad * upper * sigma * (1.0 + gate * (1.0 - sigma))).astype(BF16)
    branch = jnp.dot(activated, down_matrix, preferred_element_type=F32)
    hidden_grad = back_dot(gate_grad_r, gate_matrix) + back_dot(up_grad_r, up_matrix)
    other_branch, other_hidden_grad = swap_rows(
        members, 3, branch[rows:].astype(BF16), hidden_grad[rows:].astype(BF16)
    )
    shape = (sequence_group, token_per_shard, width)
    branch_out = (branch[:rows] + other_branch.astype(F32)).reshape(shape)
    hidden_two_grad = (hidden_grad[:rows] + other_hidden_grad.astype(F32)).reshape(shape)
    units = gate_matrix.shape[1]
    gate_wgrad = chunks(outer_sum(gate_grad_r, hid).astype(BF16), members)
    up_wgrad = chunks(outer_sum(up_grad_r, hid).astype(BF16), members)
    down_wgrad = chunks(outer_sum(activated, grads).astype(BF16), members)

    block_out = (mixed_heads + branch_out).astype(BF16)
    mlp_gain_wgrad = jnp.sum(hidden_two_grad * normed_two, axis=(0, 1))
    mixed_grad = out_grad.astype(F32) + rms_back(
        hidden_two_grad * mlp_gain_f, inv_two, normed_two
    )
    branch_grad = mixed_grad.astype(BF16)
    attn_grad = back_dot(branch_grad, output_full).astype(BF16)
    grad_parts = jnp.pad(to_groups(attn_grad, block), ((0, 0), (0, 0), (0, 0), (KV_WIDTH, 0)))
    query_back, kv_back = attend_back(
        slots, query_parts, kv_all, bias, grad_parts, mixed_parts, lse, window, block
    )
    kv_sum, gate_total, up_total, down_total = reduce_chunks(
        members,
        4,
        ((("core", "x"), False),) + ((("core", "x"), True),) * 3,
        (
            kv_back.reshape(2, 2, members, rows, 2 * KV_WIDTH),
            gate_wgrad,
            up_wgrad,
            down_wgrad,
        ),
    )
    query_grad_r = (
        rotary_inverse(
            from_groups(query_back[..., :KV_WIDTH], block).reshape(
                sequence_group, token_per_shard, QUERY_HEADS, HEAD_SIZE
            ),
            cosine_table,
            sine_table,
        )
        .reshape(sequence_group, token_per_shard, QUERY_HEADS * HEAD_SIZE)
        .astype(BF16)
    )
    kv_sum = kv_sum.reshape(sequence_group, token_per_shard, 2 * KV_WIDTH)
    key_grad_r = (
        rotary_inverse(
            kv_sum[..., :KV_WIDTH].reshape(
                sequence_group, token_per_shard, KEY_VALUE_HEADS, HEAD_SIZE
            ),
            cosine_table,
            sine_table,
        )
        .reshape(sequence_group, token_per_shard, KV_WIDTH)
        .astype(BF16)
    )
    value_grad_r = kv_sum[..., KV_WIDTH:].astype(BF16)
    hidden_one_grad = (
        back_dot(query_grad_r, query_full)
        + back_dot(key_grad_r, key_full)
        + back_dot(value_grad_r, value_full)
    )
    attn_gain_wgrad = jnp.sum(hidden_one_grad * normed_one, axis=(0, 1))
    input_grad = mixed_grad + rms_back(hidden_one_grad * attn_gain_f, inv_one, normed_one)

    part = query_matrix.shape[0]
    qkv = jnp.concatenate([query_grad_r, key_grad_r, value_grad_r], axis=-1)
    qkv_wgrad = outer_sum(qkv, hidden_one).astype(BF16)
    output_wgrad = outer_sum(branch_grad, attn_in).astype(BF16)
    both = jnp.concatenate([qkv_wgrad, output_wgrad])
    count = both.shape[0] // 2
    sides = []
    for side in range(2):
        piece = both[:, side * part : (side + 1) * part]
        sides.append(chunks(jnp.concatenate([piece[:count], piece[count:]], axis=1), members))
    small = jnp.pad(jnp.stack([attn_gain_wgrad, mlp_gain_wgrad]), ((0, 6), (0, 0)))
    attn_total, small_total = reduce_chunks(
        members,
        5,
        ((("core", "y", "x"), True),),
        (jnp.stack(sides, axis=1),),
        small,
    )
    flat = unchunk(attn_total, count)
    columns = jnp.concatenate([flat[:, :part], flat[:, part:]]).astype(F32)
    whole = columns.T
    kept = lax.dynamic_slice_in_dim(small_total, me_f * part, part, 1)
    heads = QUERY_HEADS * HEAD_SIZE
    return (
        block_out,
        input_grad,
        whole[:, :heads],
        whole[:, heads : heads + KV_WIDTH],
        whole[:, heads + KV_WIDTH : heads + 2 * KV_WIDTH],
        whole[:, heads + 2 * KV_WIDTH :],
        kept[0],
        kept[1],
        unchunk(gate_total, units).T.astype(F32),
        unchunk(up_total, units).T.astype(F32),
        unchunk(down_total, units).astype(F32),
    )


def solution(mesh):
    return jax.shard_map(
        body,
        mesh=mesh,
        in_specs=(
            P("fsdp", "ctx", None),
            P("fsdp", None),
            P("fsdp", None),
            P("fsdp", None),
            P("fsdp", None),
            P("fsdp"),
            P("fsdp"),
            P(None, "fsdp"),
            P(None, "fsdp"),
            P("fsdp", None),
            P(),
            P("fsdp", None),
            P("fsdp", "ctx", None),
        ),
        out_specs=(
            P("fsdp", "ctx", None),
            P("fsdp", "ctx", None),
            P("fsdp", None),
            P("fsdp", None),
            P("fsdp", None),
            P("fsdp", None),
            P("fsdp"),
            P("fsdp"),
            P(None, "fsdp"),
            P(None, "fsdp"),
            P("fsdp", None),
        ),
        check_vma=False,
    )
```

time: 676 us -> 276 us (0.41)
  waiting for transfers between devices: 279 us -> 0 us
  blocking collectives: 265 us -> 0 us
  Pallas kernels: 0 us -> 190 us
  matrix products: 39.3 us -> 15.7 us
  between operations: 23.1 us -> 6.89 us
    reduce_scatter x9 -> x0, waiting for transfers between devices: 276 us -> none  [the longest x1 71.8 us: body(): lax.psum_scatter(key_accumulator.reshape(sequence_group, length_value, kv...]
    pallas_call x0 -> x8, Pallas kernels: none -> 190 us  [the longest x2 122 us: reduce_chunks(): pl.pallas_call(functools.partial(reduce_kernel, members, flows, small is...]
    psum x1 -> x0, blocking collectives: 162 us -> none  [body(): lax.psum((query_part, key_portion, value_portion, output_part, attn_gain_...]
    all_gather x6 -> x0, blocking collectives: 94.6 us -> none  [the longest x1 26.6 us: body(): lax.all_gather(key_rows, 'ctx', axis=1, tiled=True)]
    dot_general x21 -> x7, matrix products: 18.9 us -> 7.07 us  [the longest x1 1.57 us: body(): jnp.dot(attn_in, output_full, preferred_element_type=F32)]
    scatter-add x4 -> x0, other arithmetic: 11 us -> none  [the longest x2 5.51 us: step(): key_running_sum.at[:, slots]]
    gather x9 -> x0, local copies, waits for them, and re-layouts: 10 us -> none  [the longest x4 7.15 us: key_slices(): jnp.take(value_blocks, slots, axis=1)]
    slice x5 -> x18, local copies, waits for them, and re-layouts: 2.29 us -> 10.7 us  [the longest x1 1.53 us: body(): columns = jnp.concatenate([flat[:, :part], flat[:, part:]]).astype(F32)]
  transfers between devices with their start and end apart: 12 -> 0, of which waited for: 9 -> 0; matrix products, arithmetic and copies ran while one was open for 9% -> 0% of each run, Pallas kernels for 0% -> 0%
where the time goes in v1:
time: 276 us; the launch traced here: 275 us
  Pallas kernels  190 us (69%)
  local copies, waits for them, and re-layouts  42.9 us (16%)
  other arithmetic  19.2 us (7%)
  matrix products  15.7 us (6%)
  between operations  6.89 us (2%)
    pallas_call x2, Pallas kernels, reduce_chunks(): pl.pallas_call(functools.partial(reduce_kernel, members, flows, small is...  122 us
    pallas_call x1, Pallas kernels, gather_keys(): pl.pallas_call(functools.partial(keys_kernel, members), out_shape=[jax.Sh...  21.8 us
    pallas_call x1, Pallas kernels, gather_weights(): pl.pallas_call(functools.partial(weights_kernel, members, count), out_sha...  19.2 us
    pallas_call x2, Pallas kernels, swap_rows(): pl.pallas_call(functools.partial(swap_kernel, members, count), out_shape=...  17.3 us
    unnamed x90, local copies, waits for them, and re-layouts  6.93 us
    pallas_call x1, Pallas kernels, attend_back(): pl.pallas_call(functools.partial(attend_back_kernel, window, block), out_...  5.54 us

profile of v1, /device:TPU:1, one launch (start us, length us, event | category | flops | bytes accessed | tf_op | source)
XLA Modules:
  0.0 275.0 jit_solution(15574763267018176027)
XLA Ops:
  3.8 19.2 %shard_map.212 = (bf16[576,576]{1,0:T(8,128)(2,1)}, bf16[576,192]{1,0:T(8,128)(2,1)}, bf16[576,192]{1,0:T(8,128)(2,1)}, bf16[576,576]{1,0:T(8,128)(2,1)}, f32[2,8,288]{2,1,0:T(8,128)}) custom-call(bf16[288,576]{1,0:T(8,128)(2,1)} %refs_0_.1, bf16[288,192]{1,0:T(8,128)(2,1)} %refs_1_.1, bf16[288,192]{1,0:T(8,128)(2,1)} %refs_2_.1, bf16[288,576]{1,0:T(8,128)(2,1)} %refs_3_.1, ...), custom_call_target="tpu_custom_call" | custom-call | tf_op jit(solution)/shard_map/pallas_call | solution.py:125
  22.9 1.4 slice_reduce_fusion
  31.4 1.3 fusion.51
  33.6 1.6 fusion.11
  36.2 1.5 copy.181
  40.0 1.8 fusion.17
  45.6 21.8 %shard_map.213 = (bf16[2,2,4,4,32,384]{5,4,3,2,1,0:T(8,128)(2,1)}, bf16[128,576]{1,0:T(8,128)(2,1)}) custom-call(bf16[4,32,384]{2,1,0:T(8,128)(2,1)} %pad_maximum_fusion.10.kv_ref, bf16[128,576]{1,0:T(8,128)(2,1)} %bitcast.120), custom_call_target="tpu_custom_call" | custom-call | tf_op jit(solution)/shard_map/pallas_call | solution.py:164
  69.8 4.1 %shard_map.214 = (f32[4,3,32,384]{3,2,1,0:T(8,128)}, f32[4,288,1]{2,1,0:T(8,128)}) custom-call(s32[20]{0:T(128)} %pad_add_fusion.1.slot_ref, bf16[4,3,32,384]{3,2,1,0:T(8,128)(2,1)} %pad.29.q_ref, bf16[16,4,32,384]{3,2,1,0:T(8,128)(2,1)} %bitcast.108, f32[4,32,160]{2,1,0:T(8,128)} %bitcast.134), custom_call_target="tpu_custom_call" | custom-call | tf_op jit(solution)/shard_map/pallas_call | solution.py:408
  73.8 1.1 slice.193
  76.3 1.6 multiply_reduce_fusion.2
  78.8 7.3 %shard_map.215 = bf16[128,576]{1,0:T(8,128)(2,1)} custom-call(bf16[128,576]{1,0:T(8,128)(2,1)} %bitcast.110), custom_call_target="tpu_custom_call" | custom-call | tf_op jit(solution)/shard_map/pallas_call | solution.py:190
  86.1 1.5 fusion.56
  88.2 1.4 multiply_convert_fusion
  90.7 1.4 fusion.66
  94.6 10.0 %shard_map.216 = (bf16[128,576]{1,0:T(8,128)(2,1)}, bf16[128,576]{1,0:T(8,128)(2,1)}) custom-call(bf16[128,576]{1,0:T(8,128)(2,1)} %copy.189.refs_0_, bf16[128,576]{1,0:T(8,128)(2,1)} %copy.192.refs_1_), custom_call_target="tpu_custom_call" | custom-call | tf_op jit(solution)/shard_map/pallas_call | solution.py:190
  108.5 5.5 %shard_map.217 = (f32[4,3,32,384]{3,2,1,0:T(8,128)}, bf16[16,4,32,384]{3,2,1,0:T(8,128)(2,1)}) custom-call(s32[20]{0:T(128)} %pad_add_fusion.1.slot_ref, bf16[4,3,32,384]{3,2,1,0:T(8,128)(2,1)} %pad.29.q_ref, bf16[16,4,32,384]{3,2,1,0:T(8,128)(2,1)} %bitcast.109, f32[4,32,160]{2,1,0:T(8,128)} %bitcast.135, bf16[4,3,32,384]{3,2,1,0:T(8,128)(2,1)} %pad.31.grad_ref, ...), custom_call_target="tpu_custom_call" | custom-call | tf_op jit(solution)/shard_map/pallas_call | solution.py:451
  116.9 2.0 copy.159
  123.4 1.3 copy.160
  125.1 1.3 copy.161
  126.5 1.4 convolution_convert_fusion
  127.8 1.3 copy.162
  129.2 71.3 %shard_map.218 = (f32[128,384]{1,0:T(8,128)}, bf16[2,2,4,48,576]{4,3,2,1,0:T(8,128)(2,1)}, bf16[2,2,4,48,576]{4,3,2,1,0:T(8,128)(2,1)}, bf16[2,2,4,48,576]{4,3,2,1,0:T(8,128)(2,1)}) custom-call(bf16[2,2,4,128,384]{4,3,2,1,0:T(8,128)(2,1)} %bitcast.128, bf16[2,2,4,48,576]{4,3,2,1,0:T(8,128)(2,1)} %bitcast.115, bf16[2,2,4,48,576]{4,3,2,1,0:T(8,128)(2,1)} %bitcast.116, ...), custom_call_target="tpu_custom_call" | custom-call | tf_op jit(solution)/shard_map/pallas_call | solution.py:337
  202.1 1.3 fusion.23
  208.7 1.6 pad_maximum_fusion.refs_0_
  211.0 51.1 %shard_map.219 = (bf16[2,2,4,48,576]{4,3,2,1,0:T(8,128)(2,1)}, f32[8,576]{1,0:T(8,128)}) custom-call(bf16[2,2,2,4,48,576]{5,4,3,2,1,0:T(8,128)(2,1)} %pad_maximum_fusion.refs_0_, f32[8,576]{1,0:T(8,128)} %select_maximum_fusion.refs_1_), custom_call_target="tpu_custom_call" | custom-call | tf_op jit(solution)/shard_map/pallas_call | solution.py:337
  262.1 1.5 fusion.61
  264.3 1.3 fusion.58
  266.5 1.5 dynamic-slice_reduce_fusion
  268.2 1.7 copy.173
  270.1 1.7 copy.174
  271.9 1.4 bitcast_convert_fusion.1
  273.3 1.7 copy.175
  (202 shorter events, 42.0 us)
Async XLA Ops:
  0.6 87.5 %copy-start = (bf16[768,576]{0,1:T(8,128)(2,1)S(1)}, bf16[768,576]{0,1:T(8,128)(2,1)}, u32[]{:S(2)}) copy-start(bf16[768,576]{0,1:T(8,128)(2,1)} %param.22) | copy-start | bytes 2654212
  33.0 6.9 %copy-start.30 = (f32[64,64]{1,0:T(8,128)}, f32[64,64]{1,0:T(8,128)S(1)}, u32[]{:S(2)}) copy-start(f32[64,64]{1,0:T(8,128)S(1)} %get-tuple-element.141) | copy-start | bytes 49156
  33.0 10.9 %copy-start.25 = (f32[64,64]{1,0:T(8,128)}, f32[64,64]{1,0:T(8,128)S(1)}, u32[]{:S(2)}) copy-start(f32[64,64]{1,0:T(8,128)S(1)} %get-tuple-element.142) | copy-start | bytes 49156
  38.4 1.5 copy-start.34
  39.9 3.1 %copy-start.2 = (bf16[2,64,576]{2,1,0:T(8,128)(2,1)S(1)}, bf16[2,64,576]{2,1,0:T(8,128)(2,1)}, u32[]{:S(2)}) copy-start(bf16[2,64,576]{2,1,0:T(8,128)(2,1)} %param.13) | copy-start | bytes 442372
  39.9 3.1 %copy-start.27 = (bf16[576,192]{1,0:T(8,128)(2,1)S(1)}, bf16[576,192]{1,0:T(8,128)(2,1)}, u32[]{:S(2)}) copy-start(bf16[576,192]{1,0:T(8,128)(2,1)} %get-tuple-element.33) | copy-start | bytes 663556
  41.8 1.5 copy-start.20
  42.2 2.4 copy-start.31
  43.3 25.5 %copy-start.36 = (s32[2,1024]{1,0:T(2,128)S(1)}, s32[2,1024]{1,0:T(2,128)}, u32[]{:S(2)}) copy-start(s32[2,1024]{1,0:T(2,128)} %param.24) | copy-start | bytes 24580
  44.7 29.1 %copy-start.28 = (f32[64,64]{0,1:T(8,128)}, f32[64,64]{0,1:T(8,128)S(1)}, u32[]{:S(2)}) copy-start(f32[64,64]{0,1:T(8,128)S(1)} %copy.141) | copy-start | bytes 49156
  73.8 4.1 %copy-start.38 = (f32[2,288]{1,0:T(2,128)S(1)}, f32[2,288]{1,0:T(2,128)}, u32[]{:S(2)}) copy-start(f32[2,288]{1,0:T(2,128)} %get-tuple-element.97) | copy-start | bytes 6916
  75.1 11.0 %copy-start.5 = (bf16[576,768]{1,0:T(8,128)(2,1)S(1)}, bf16[576,768]{1,0:T(8,128)(2,1)}, u32[]{:S(2)}) copy-start(bf16[576,768]{1,0:T(8,128)(2,1)} %param.20) | copy-start | bytes 2654212
  76.3 11.4 %copy-start.6 = (bf16[576,768]{1,0:T(8,128)(2,1)S(1)}, bf16[576,768]{1,0:T(8,128)(2,1)}, u32[]{:S(2)}) copy-start(bf16[576,768]{1,0:T(8,128)(2,1)} %param.21) | copy-start | bytes 2654212
  78.8 8.9 %copy-start.3 = (bf16[2,64,576]{2,1,0:T(8,128)(2,1)S(1)}, bf16[2,64,576]{2,1,0:T(8,128)(2,1)}, u32[]{:S(2)}) copy-start(bf16[2,64,576]{2,1,0:T(8,128)(2,1)} %multiply_convert_fusion.3) | copy-start | bytes 442372
  86.1 1.6 copy-start.4
  86.1 2.1 copy-start.11
  86.1 2.1 copy-start.35
  93.0 13.4 %copy-start.12 = (bf16[2,64,576]{2,1,0:T(8,128)(2,1)S(1)}, bf16[2,64,576]{2,1,0:T(8,128)(2,1)}, u32[]{:S(2)}) copy-start(bf16[2,64,576]{2,1,0:T(8,128)(2,1)} %param.25) | copy-start | bytes 442372
  93.8 12.7 %copy-start.10 = (bf16[576,576]{1,0:T(8,128)(2,1)S(1)}, bf16[576,576]{1,0:T(8,128)(2,1)}, u32[]{:S(2)}) copy-start(bf16[576,576]{1,0:T(8,128)(2,1)} %get-tuple-element.36) | copy-start | bytes 1990660
  116.9 3.5 %copy-start.29 = (f32[64,64]{0,1:T(8,128)S(1)}, f32[64,64]{0,1:T(8,128)}, u32[]{:S(2)}) copy-start(f32[64,64]{0,1:T(8,128)} %copy-done.28) | copy-start | bytes 49156
  119.4 2.4 copy-start.9
  120.5 2.4 copy-start.18
  122.9 1.8 copy-start.16
  124.7 1.8 copy-start.14
  129.2 72.4 %copy-start.33 = (f32[64,64]{0,1:T(8,128)S(1)}, f32[64,64]{0,1:T(8,128)}, u32[]{:S(2)}) copy-start(f32[64,64]{0,1:T(8,128)} %copy-done.32) | copy-start | bytes 49156
  201.7 1.8 slice-start
  202.1 2.5 copy-start.40
  203.5 2.1 copy-start.8
  208.7 1.6 copy-start.37
  264.3 3.7 %copy-start.24 = (bf16[2,2,4,48,576]{4,3,2,1,0:T(8,128)(2,1)S(1)}, bf16[2,2,4,48,576]{4,3,2,1,0:T(8,128)(2,1)}, u32[]{:S(2)}) copy-start(bf16[2,2,4,48,576]{4,3,2,1,0:T(8,128)(2,1)} %get-tuple-element.46) | copy-start | bytes 2654212
  268.2 1.7 copy-start.23
  271.8 3.1 %copy-start.1 = (bf16[768,576]{0,1:T(8,128)(2,1)S(1)}, bf16[768,576]{0,1:T(8,128)(2,1)}, u32[]{:S(2)}) copy-start(bf16[768,576]{0,1:T(8,128)(2,1)} %param.22) | copy-start | bytes 2654212
  (10 other events, 10.7 us)

commit v2 on v1

--- a/solution.py
+++ b/solution.py
@@ -133,45 +133,61 @@
     )(*weights, gains)
 
 
-def keys_kernel(members, kv_ref, grad_ref, out_ref, other_ref, send, recv):
+def keys_kernel(
+    members, kv_ref, grad_ref, w_ref, out_ref, other_ref, full_ref, send, recv
+):
     me = Place(members)
     me.greet(("core", "x", "y"), True)
     sems = Sems(send, recv)
+    rows = w_ref.shape[0]
+    half = rows // 2
     mine = out_ref.at[me.core, me.x, me.far]
     far = [sems.copy(kv_ref, mine, me.far_device(step)) for step in range(1, members)]
     own = sems.copy(kv_ref, mine, me.partner("x"))
+    put = pl.ds(pl.multiple_of(me.fsdp * rows + me.core * half, 16), half)
+    weight = sems.copy(
+        w_ref.at[pl.ds(pl.multiple_of(me.core * half, 16), half)],
+        full_ref.at[put],
+        me.partner("y"),
+    )
     swap = sems.copy(grad_ref, other_ref, me.partner("y"))
     out_ref[me.core, me.x, me.far] = kv_ref[...]
+    full_ref[pl.ds(pl.multiple_of(me.fsdp * rows, 16), rows)] = w_ref[...]
     along = []
     for step in range(1, members):
         far[step - 1].wait_recv()
         got = out_ref.at[me.core, me.x, me.far_member(members - step)]
         along.append(sems.copy(got, got, me.partner("x")))
+    weight.wait_recv()
+    put = pl.ds(pl.multiple_of((1 - me.fsdp) * rows + me.core * half, 16), half)
+    across = sems.copy(full_ref.at[put], full_ref.at[put], me.partner("core"))
+    block = out_ref.at[me.core, me.x]
+    near = sems.copy(block, block, me.partner("core"))
     own.wait_recv()
     for copy in along:
         copy.wait_recv()
-    block = out_ref.at[me.core]
+    block = out_ref.at[me.core, 1 - me.x]
     last = sems.copy(block, block, me.partner("core"))
-    last.wait()
-    swap.wait()
-    own.wait_send()
-    for copy in far + along:
+    for copy in (near, last, across, swap):
+        copy.wait()
+    for copy in far + along + [own, weight]:
         copy.wait_send()
 
 
-def gather_keys(members, kv, grad):
-    count = 2 * (members - 1) + 3
+def gather_keys(members, kv, grad, weight):
+    count = 2 * (members - 1) + 6
     return pl.pallas_call(
         functools.partial(keys_kernel, members),
         out_shape=[
             jax.ShapeDtypeStruct((2, 2, members) + kv.shape, kv.dtype),
             jax.ShapeDtypeStruct(grad.shape, grad.dtype),
+            jax.ShapeDtypeStruct((2 * weight.shape[0], weight.shape[1]), weight.dtype),
         ],
-        in_specs=[VMEM] * 2,
-        out_specs=[VMEM] * 2,
+        in_specs=[VMEM] * 3,
+        out_specs=[VMEM] * 3,
         scratch_shapes=[pltpu.SemaphoreType.DMA((count,))] * 2,
         compiler_params=params(1),
-    )(kv, grad)
+    )(kv, grad, weight)
 
 
 def swap_kernel(members, count, *refs):
@@ -201,21 +217,19 @@
     return (a.astype(F32) + b.astype(F32)).astype(BF16)
 
 
-def reduce_kernel(members, flows, has_small, *refs):
+def reduce_kernel(members, kinds, flows, has_small, *refs):
     refs = list(refs)
-    ins = [refs.pop(0) for _ in flows]
+    ins = [refs.pop(0) for _ in kinds]
     small_in = refs.pop(0) if has_small else None
-    outs = [refs.pop(0) for _ in flows]
+    outs = [refs.pop(0) for _ in kinds]
     small_out = refs.pop(0) if has_small else None
-    gots = [[refs.pop(0) for _ in axes] for axes, _ in flows]
+    gots = [[refs.pop(0) for _ in kinds[array][0]] for array, _, _ in flows]
     far_gots = [refs.pop(0) for _ in flows]
     axes_all = []
-    for axes, _ in flows:
+    for axes, _ in kinds:
         axes_all += [axis for axis in axes if axis not in axes_all]
     if has_small:
-        small_acc = refs.pop(0)
-        small_got = refs.pop(0)
-        small_far = refs.pop(0)
+        small_acc, small_got, small_far = [refs.pop(0) for _ in range(3)]
     send, recv = refs
     me = Place(members)
     me.greet(tuple(axes_all), True)
@@ -227,105 +241,115 @@
         sent.append(copy)
         return copy
 
-    flying = []
-    for f, (axes, _) in enumerate(flows):
-        flying.append(
-            go(ins[f].at[1 - me.own(axes[0])], gots[f][0], me.partner(axes[0]))
-        )
-    depth = max(len(axes) for axes, _ in flows)
-    far_flying = [None] * len(flows)
-    small = None
-    if has_small:
-        small_acc[0] = small_in[...]
-        small = go(small_acc.at[0], small_got.at[0], me.partner(axes_all[0]))
-    for level in range(depth):
-        for f, (axes, _) in enumerate(flows):
-            if level >= len(axes):
-                continue
-            flying[f].wait_recv()
-            source = ins[f] if level == 0 else gots[f][level - 1]
-            held = source.at[me.own(axes[level])]
-            got = total = gots[f][level]
+    def steps(f):
+        array, low, rows = flows[f]
+        axes, gather = kinds[array]
+        cut = pl.ds(low, rows)
+
+        def part(index):
+            return ins[array].at[(index,) + (slice(None),) * len(axes) + (cut,)]
+
+        flying = go(part(1 - me.own(axes[0])), gots[f][0], me.partner(axes[0]))
+        yield
+        for level, axis in enumerate(axes):
+            flying.wait_recv()
+            held = part(me.own(axis)) if level == 0 else gots[f][level - 1].at[me.own(axis)]
+            got = gots[f][level]
             if level + 1 < len(axes):
-                away = 1 - me.own(axes[level + 1])
                 keep = me.own(axes[level + 1])
-                total[away] = add(held[away], got[away])
-                flying[f] = go(
-                    total.at[away], gots[f][level + 1], me.partner(axes[level + 1])
-                )
-                total[keep] = add(held[keep], got[keep])
+                away = 1 - keep
+                got[away] = add(held[away], got[away])
+                flying = go(got.at[away], gots[f][level + 1], me.partner(axes[level + 1]))
+                got[keep] = add(held[keep], got[keep])
             else:
-                far_flying[f] = []
+                spread_out = []
                 for step in range(1, members):
                     to = me.far_member(step)
-                    total[to] = add(held[to], got[to])
-                    far_flying[f].append(
-                        go(total.at[to], far_gots[f].at[step - 1], me.far_device(step))
+                    got[to] = add(held[to], got[to])
+                    spread_out.append(
+                        go(got.at[to], far_gots[f].at[step - 1], me.far_device(step))
                     )
-                total[me.far] = add(held[me.far], got[me.far])
-        if has_small:
-            small.wait_recv()
-            small_acc[level + 1] = small_acc[level] + small_got[level]
-            if level + 1 < depth:
-                small = go(
-                    small_acc.at[level + 1],
-                    small_got.at[level + 1],
-                    me.partner(axes_all[level + 1]),
-                )
-            else:
-                small = [
-                    go(small_acc.at[level + 1], small_far.at[step - 1], me.far_device(step))
-                    for step in range(1, members)
-                ]
-    back = [None] * len(flows)
-    for f, (axes, gather) in enumerate(flows):
+                got[me.far] = add(held[me.far], got[me.far])
+            yield
         whole = gots[f][-1][me.far].astype(F32)
         for step in range(1, members):
-            far_flying[f][step - 1].wait_recv()
+            spread_out[step - 1].wait_recv()
             whole = whole + far_gots[f][step - 1].astype(F32)
         if not gather:
-            outs[f][...] = whole
-            continue
-        outs[f][me.core, me.x, me.far] = whole.astype(BF16)
-        mine = outs[f].at[me.core, me.x, me.far]
-        back[f] = [go(mine, mine, me.far_device(step)) for step in range(1, members)]
-    if has_small:
+            outs[array][cut] = whole
+            return
+        outs[array][me.core, me.x, me.far, cut] = whole.astype(BF16)
+        mine = outs[array].at[me.core, me.x, me.far, cut]
+        back = [go(mine, mine, me.far_device(step)) for step in range(1, members)]
+        yield
+        for copy in back:
+            copy.wait_recv()
+        block = outs[array].at[me.core, me.x, :, cut]
+        flying = go(block, block, me.partner("x"))
+        yield
+        flying.wait_recv()
+        block = outs[array].at[me.core, :, :, cut]
+        flying = go(block, block, me.partner("core"))
+        yield
+        flying.wait_recv()
+
+    def small_steps():
+        depth = len(axes_all)
+        small_acc[0] = small_in[...]
+        for level in range(depth):
+            flying = go(small_acc.at[level], small_got.at[level], me.partner(axes_all[level]))
+            yield
+            flying.wait_recv()
+            small_acc[level + 1] = small_acc[level] + small_got[level]
+        last = [
+            go(small_acc.at[depth], small_far.at[step - 1], me.far_device(step))
+            for step in range(1, members)
+        ]
+        yield
         whole = small_acc[depth]
         for step in range(1, members):
-            small[step - 1].wait_recv()
+            last[step - 1].wait_recv()
             whole = whole + small_far[step - 1]
         small_out[...] = whole
-    for axis in ("x", "core"):
-        for f, (axes, gather) in enumerate(flows):
-            if gather:
-                for copy in back[f]:
-                    copy.wait_recv()
-                block = outs[f].at[me.core, me.x] if axis == "x" else outs[f].at[me.core]
-                back[f] = [go(block, block, me.partner(axis))]
-    for f, (axes, gather) in enumerate(flows):
-        if gather:
-            back[f][0].wait_recv()
+
+    line = [steps(f) for f in range(len(flows))]
+    starts = [max(0, f - 2) for f in range(len(flows))]
+    if has_small:
+        line.append(small_steps())
+        starts.append(0)
+    live, now = set(range(len(line))), 0
+    while live:
+        for f in sorted(live):
+            if now >= starts[f] and next(line[f], True):
+                live.discard(f)
+        now += 1
     for copy in sent:
         copy.wait_send()
 
 
-def reduce_chunks(members, collective_id, flows, arrays, small=None):
-    flows = tuple((tuple(axes), gather) for axes, gather in flows)
-    outs, gots, fars, count = [], [], [], 0
-    for (axes, gather), array in zip(flows, arrays):
+def reduce_chunks(members, collective_id, kinds, arrays, pieces, small=None):
+    kinds = tuple((tuple(axes), gather) for axes, gather in kinds)
+    outs, gots, fars, flows, count = [], [], [], [], 0
+    for at, ((axes, gather), array) in enumerate(zip(kinds, arrays)):
         chunk = array.shape[len(axes) + 1 :]
         if gather:
             outs.append(jax.ShapeDtypeStruct((2, 2, members) + chunk, array.dtype))
         else:
             outs.append(jax.ShapeDtypeStruct(chunk, F32))
-        for level in range(len(axes)):
-            gots.append(pltpu.VMEM(array.shape[level + 1 :], array.dtype))
-        fars.append(pltpu.VMEM((members - 1,) + chunk, array.dtype))
-        count += len(axes) + members - 1 + (members + 1 if gather else 0)
-    depth = max(len(axes) for axes, _ in flows)
+        low = 0
+        while low < chunk[0]:
+            rows = min(pieces, chunk[0] - low)
+            flows.append((at, low, rows))
+            low += rows
+            for level in range(len(axes)):
+                lead = array.shape[level + 1 : len(axes) + 1]
+                gots.append(pltpu.VMEM(lead + (rows,) + chunk[1:], array.dtype))
+            fars.append(pltpu.VMEM((members - 1, rows) + chunk[1:], array.dtype))
+            count += len(axes) + members - 1 + (members + 1 if gather else 0)
     scratch = gots + fars
     operands = list(arrays)
     if small is not None:
+        depth = max(len(axes) for axes, _ in kinds)
         outs.append(jax.ShapeDtypeStruct(small.shape, small.dtype))
         scratch += [
             pltpu.VMEM((depth + 1,) + small.shape, small.dtype),
@@ -335,7 +359,7 @@
         operands.append(small)
         count += depth + members - 1
     return pl.pallas_call(
-        functools.partial(reduce_kernel, members, flows, small is not None),
+        functools.partial(reduce_kernel, members, kinds, tuple(flows), small is not None),
         out_shape=outs,
         in_specs=[VMEM] * len(operands),
         out_specs=[VMEM] * len(outs),
@@ -554,8 +578,8 @@
     gains = jnp.pad(
         jnp.stack([attn_gain, mlp_gain]).astype(F32), ((0, 6), (0, 0))
     )
-    query_full, key_full, value_full, output_full, gains_full = gather_weights(
-        members, (query_matrix, key_projection, value_projection, output_matrix), gains
+    query_full, key_full, value_full, gains_full = gather_weights(
+        members, (query_matrix, key_projection, value_projection), gains
     )
     attn_gain_f = gains_full[:, 0].reshape(width)
     mlp_gain_f = gains_full[:, 1].reshape(width)
@@ -610,7 +634,9 @@
         2 * sequence_group, block, 2 * KV_WIDTH
     )
     flat_grad = out_grad.reshape(rows, width)
-    kv_all, other_grad = gather_keys(members, own_kv, flat_grad)
+    kv_all, other_grad, output_full = gather_keys(
+        members, own_kv, flat_grad, output_matrix
+    )
     kv_all = kv_all.reshape(pairs, 2 * sequence_group, block, 2 * KV_WIDTH)
 
     query_parts = jnp.pad(to_groups(query_rows, block), ((0, 0), (0, 0), (0, 0), (0, KV_WIDTH)))
@@ -655,16 +681,12 @@
     query_back, kv_back = attend_back(
         slots, query_parts, kv_all, bias, grad_parts, mixed_parts, lse, window, block
     )
-    kv_sum, gate_total, up_total, down_total = reduce_chunks(
+    (kv_sum,) = reduce_chunks(
         members,
         4,
-        ((("core", "x"), False),) + ((("core", "x"), True),) * 3,
-        (
-            kv_back.reshape(2, 2, members, rows, 2 * KV_WIDTH),
-            gate_wgrad,
-            up_wgrad,
-            down_wgrad,
-        ),
+        ((("core", "x"), False),),
+        (kv_back.reshape(2, 2, members, rows, 2 * KV_WIDTH),),
+        rows // 2,
     )
     query_grad_r = (
         rotary_inverse(
@@ -709,11 +731,12 @@
         piece = both[:, side * part : (side + 1) * part]
         sides.append(chunks(jnp.concatenate([piece[:count], piece[count:]], axis=1), members))
     small = jnp.pad(jnp.stack([attn_gain_wgrad, mlp_gain_wgrad]), ((0, 6), (0, 0)))
-    attn_total, small_total = reduce_chunks(
+    attn_total, gate_total, up_total, down_total, small_total = reduce_chunks(
         members,
         5,
-        ((("core", "y", "x"), True),),
-        (jnp.stack(sides, axis=1),),
+        ((("core", "y", "x"), True),) + ((("core", "x"), True),) * 3,
+        (jnp.stack(sides, axis=1), gate_wgrad, up_wgrad, down_wgrad),
+        32,
         small,
     )
     flat = unchunk(attn_total, count)

time: 276 us -> 260 us (0.942)
  Pallas kernels: 190 us -> 167 us
  local copies, waits for them, and re-layouts: 42.9 us -> 46.6 us
  matrix products: 15.7 us -> 18.9 us
    pallas_call x2, Pallas kernels: 122 us -> 103 us  [reduce_chunks(): pl.pallas_call(functools.partial(reduce_kernel, members, kinds, tuple(flo...]
    pallas_call x1, Pallas kernels: 19.2 us -> 14.7 us  [gather_weights(): pl.pallas_call(functools.partial(weights_kernel, members, count), out_sha...]
    dot_general x5, matrix products: 3.23 us -> 6.29 us  [outer_sum(): lax.dot_general(flat_left, flat_right, (((0,), (0,)), ((), ())), preferre...]
    unnamed x90 -> x88, local copies, waits for them, and re-layouts: 6.93 us -> 7.06 us
where the time goes in v2:
time: 260 us; the launch traced here: 259 us
  Pallas kernels  167 us (64%)
  local copies, waits for them, and re-layouts  46.6 us (18%)
  other arithmetic  19.9 us (8%)
  matrix products  18.9 us (7%)
  between operations  6.88 us (3%)
    pallas_call x2, Pallas kernels, reduce_chunks(): pl.pallas_call(functools.partial(reduce_kernel, members, kinds, tuple(flo...  103 us
    pallas_call x1, Pallas kernels, gather_keys(): pl.pallas_call(functools.partial(keys_kernel, members), out_shape=[jax.Sh...  21.7 us
    pallas_call x2, Pallas kernels, swap_rows(): pl.pallas_call(functools.partial(swap_kernel, members, count), out_shape=...  17.4 us
    pallas_call x1, Pallas kernels, gather_weights(): pl.pallas_call(functools.partial(weights_kernel, members, count), out_sha...  14.7 us
    unnamed x88, local copies, waits for them, and re-layouts  7.06 us
    dot_general x5, matrix products, outer_sum(): lax.dot_general(flat_left, flat_right, (((0,), (0,)), ((), ())), preferre...  6.29 us
    dot_general x7, matrix products, back_dot(): lax.dot_general(grads, weight, (((grads.ndim - 1,), (1,)), ((), ())), pre...  5.81 us
    pallas_call x1, Pallas kernels, attend_back(): pl.pallas_call(functools.partial(attend_back_kernel, window, block), out_...  5.54 us

profile of v2, /device:TPU:1, one launch (start us, length us, event | category | flops | bytes accessed | tf_op | source)
XLA Modules:
  0.0 258.8 jit_solution(4319524881725312597)
XLA Ops:
  7.2 1.3 fusion.51
  18.6 14.7 %shard_map.212 = (bf16[576,576]{1,0:T(8,128)(2,1)}, bf16[576,192]{1,0:T(8,128)(2,1)}, bf16[576,192]{1,0:T(8,128)(2,1)}, f32[2,8,288]{2,1,0:T(8,128)}) custom-call(bf16[288,576]{1,0:T(8,128)(2,1)} %refs_0_.1, bf16[288,192]{1,0:T(8,128)(2,1)} %refs_1_.1, bf16[288,192]{1,0:T(8,128)(2,1)} %refs_2_.1, f32[8,288]{1,0:T(8,128)} %fusion.43.refs_3_), custom_call_target="tpu_custom_call" | custom-call | tf_op jit(solution)/shard_map/pallas_call | solution.py:125
  38.5 1.2 reshape.216
  42.1 2.0 fusion.17
  45.4 21.7 %shard_map.213 = (bf16[2,2,4,4,32,384]{5,4,3,2,1,0:T(8,128)(2,1)}, bf16[128,576]{1,0:T(8,128)(2,1)}, bf16[576,576]{1,0:T(8,128)(2,1)}) custom-call(bf16[4,32,384]{2,1,0:T(8,128)(2,1)} %pad_maximum_fusion.10.kv_ref, bf16[128,576]{1,0:T(8,128)(2,1)} %bitcast.120, bf16[288,576]{1,0:T(8,128)(2,1)} %w_ref.1), custom_call_target="tpu_custom_call" | custom-call | tf_op jit(solution)/shard_map/pallas_call | solution.py:179
  67.1 4.1 %shard_map.214 = (f32[4,3,32,384]{3,2,1,0:T(8,128)}, f32[4,288,1]{2,1,0:T(8,128)}) custom-call(s32[20]{0:T(128)} %pad_add_fusion.1.slot_ref, bf16[4,3,32,384]{3,2,1,0:T(8,128)(2,1)} %pad.29.q_ref, bf16[16,4,32,384]{3,2,1,0:T(8,128)(2,1)} %bitcast.108, f32[4,32,160]{2,1,0:T(8,128)} %bitcast.138), custom_call_target="tpu_custom_call" | custom-call | tf_op jit(solution)/shard_map/pallas_call | solution.py:432
  74.1 1.6 multiply_reduce_fusion.2
  76.4 7.3 %shard_map.215 = bf16[128,576]{1,0:T(8,128)(2,1)} custom-call(bf16[128,576]{1,0:T(8,128)(2,1)} %bitcast.110), custom_call_target="tpu_custom_call" | custom-call | tf_op jit(solution)/shard_map/pallas_call | solution.py:206
  83.8 1.5 fusion.55
  85.9 1.5 multiply_convert_fusion
  90.4 1.6 convolution_convert_fusion
  92.0 1.5 copy.170
  93.5 1.5 fusion.67
  96.3 10.1 %shard_map.216 = (bf16[128,576]{1,0:T(8,128)(2,1)}, bf16[128,576]{1,0:T(8,128)(2,1)}) custom-call(bf16[128,576]{1,0:T(8,128)(2,1)} %copy.189.refs_0_, bf16[128,576]{1,0:T(8,128)(2,1)} %copy.192.refs_1_), custom_call_target="tpu_custom_call" | custom-call | tf_op jit(solution)/shard_map/pallas_call | solution.py:206
  106.3 1.7 convert_add_fusion.1
  112.2 5.5 %shard_map.217 = (f32[4,3,32,384]{3,2,1,0:T(8,128)}, bf16[16,4,32,384]{3,2,1,0:T(8,128)(2,1)}) custom-call(s32[20]{0:T(128)} %pad_add_fusion.1.slot_ref, bf16[4,3,32,384]{3,2,1,0:T(8,128)(2,1)} %pad.29.q_ref, bf16[16,4,32,384]{3,2,1,0:T(8,128)(2,1)} %bitcast.109, f32[4,32,160]{2,1,0:T(8,128)} %bitcast.139, bf16[4,3,32,384]{3,2,1,0:T(8,128)(2,1)} %pad.31.grad_ref, ...), custom_call_target="tpu_custom_call" | custom-call | tf_op jit(solution)/shard_map/pallas_call | solution.py:475
  118.7 23.4 %shard_map.218 = f32[128,384]{1,0:T(8,128)} custom-call(bf16[2,2,4,128,384]{4,3,2,1,0:T(8,128)(2,1)} %bitcast.132), custom_call_target="tpu_custom_call" | custom-call | tf_op jit(solution)/shard_map/pallas_call | solution.py:361
  142.2 1.7 slice.195
  145.7 1.3 convolution_convert_fusion.3
  147.0 1.4 convolution_convert_fusion.1
  148.4 1.3 copy.169
  149.7 1.4 convolution_convert_fusion.2
  151.2 1.3 copy.168
  164.6 1.6 pad_maximum_fusion.refs_0_
  166.2 79.7 %shard_map.219 = (bf16[2,2,4,48,576]{4,3,2,1,0:T(8,128)(2,1)}, bf16[2,2,4,48,576]{4,3,2,1,0:T(8,128)(2,1)}, bf16[2,2,4,48,576]{4,3,2,1,0:T(8,128)(2,1)}, bf16[2,2,4,48,576]{4,3,2,1,0:T(8,128)(2,1)}, f32[8,576]{1,0:T(8,128)}) custom-call(bf16[2,2,2,4,48,576]{5,4,3,2,1,0:T(8,128)(2,1)} %pad_maximum_fusion.refs_0_, bf16[2,2,4,48,576]{4,3,2,1,0:T(8,128)(2,1)} %bitcast.117, ...), custom_call_target="tpu_custom_call" | custom-call | tf_op jit(solution)/shard_map/pallas_call | solution.py:361
  245.9 1.5 dynamic-slice_reduce_fusion
  247.4 1.5 fusion.61
  250.5 1.3 fusion.58
  252.1 1.7 copy.173
  254.0 1.7 copy.174
  255.7 1.4 bitcast_convert_fusion.1
  257.1 1.7 copy.175
  (199 shorter events, 49.1 us)
Async XLA Ops:
  0.6 85.2 %copy-start = (bf16[768,576]{0,1:T(8,128)(2,1)S(1)}, bf16[768,576]{0,1:T(8,128)(2,1)}, u32[]{:S(2)}) copy-start(bf16[768,576]{0,1:T(8,128)(2,1)} %param.22) | copy-start | bytes 2654212
  0.7 33.7 %copy-start.2 = (bf16[2,64,576]{2,1,0:T(8,128)(2,1)S(1)}, bf16[2,64,576]{2,1,0:T(8,128)(2,1)}, u32[]{:S(2)}) copy-start(bf16[2,64,576]{2,1,0:T(8,128)(2,1)} %param.13) | copy-start | bytes 442372
  9.6 28.2 %copy-start.33 = (f32[2,64]{1,0:T(2,128)}, f32[2,64]{1,0:T(2,128)S(1)}, u32[]{:S(2)}) copy-start(f32[2,64]{1,0:T(2,128)S(1)} %add_rsqrt_fusion.1) | copy-start | bytes 1540
  17.0 20.1 %copy-start.22 = (f32[64,192]{1,0:T(8,128)}, f32[64,192]{1,0:T(8,128)S(1)}, u32[]{:S(2)}) copy-start(f32[64,192]{1,0:T(8,128)S(1)} %copy.142) | copy-start | bytes 147460
  33.3 4.5 %copy-start.8 = (bf16[576,576]{1,0:T(8,128)(2,1)S(1)}, bf16[576,576]{1,0:T(8,128)(2,1)}, u32[]{:S(2)}) copy-start(bf16[576,576]{1,0:T(8,128)(2,1)} %get-tuple-element.30) | copy-start | bytes 1990660
  34.2 75.8 %copy-start.31 = (f32[576]{0:T(1024)}, f32[576]{0:T(1024)S(1)}, u32[]{:S(2)}) copy-start(f32[576]{0:T(1024)S(1)} %mul.287) | copy-start | bytes 6916
  34.3 3.9 %copy-start.29 = (f32[576]{0:T(1024)}, f32[576]{0:T(1024)S(1)}, u32[]{:S(2)}) copy-start(f32[576]{0:T(1024)S(1)} %mul.259) | copy-start | bytes 6916
  40.5 1.7 copy-start.26
  40.5 1.7 copy-start.27
  72.8 11.0 %copy-start.6 = (bf16[576,768]{1,0:T(8,128)(2,1)S(1)}, bf16[576,768]{1,0:T(8,128)(2,1)}, u32[]{:S(2)}) copy-start(bf16[576,768]{1,0:T(8,128)(2,1)} %param.21) | copy-start | bytes 2654212
  74.1 11.3 %copy-start.5 = (bf16[576,768]{1,0:T(8,128)(2,1)S(1)}, bf16[576,768]{1,0:T(8,128)(2,1)}, u32[]{:S(2)}) copy-start(bf16[576,768]{1,0:T(8,128)(2,1)} %param.20) | copy-start | bytes 2654212
  75.7 34.3 %copy-start.35 = (f32[2,64]{1,0:T(2,128)}, f32[2,64]{1,0:T(2,128)S(1)}, u32[]{:S(2)}) copy-start(f32[2,64]{1,0:T(2,128)S(1)} %add_rsqrt_fusion) | copy-start | bytes 1540
  76.4 8.9 %copy-start.3 = (bf16[2,64,576]{2,1,0:T(8,128)(2,1)S(1)}, bf16[2,64,576]{2,1,0:T(8,128)(2,1)}, u32[]{:S(2)}) copy-start(bf16[2,64,576]{2,1,0:T(8,128)(2,1)} %multiply_convert_fusion.3) | copy-start | bytes 442372
  83.8 1.6 copy-start.4
  83.8 2.1 copy-start.11
  83.8 2.1 copy-start.28
  94.9 11.4 %copy-start.16 = (f32[128,576]{1,0:T(8,128)S(1)}, f32[128,576]{1,0:T(8,128)}, u32[]{:S(2)}) copy-start(f32[128,576]{1,0:T(8,128)} %copy.188) | copy-start | bytes 884740
  96.3 13.7 %copy-start.12 = (bf16[2,64,576]{2,1,0:T(8,128)(2,1)S(1)}, bf16[2,64,576]{2,1,0:T(8,128)(2,1)}, u32[]{:S(2)}) copy-start(bf16[2,64,576]{2,1,0:T(8,128)(2,1)} %param.25) | copy-start | bytes 442372
  108.0 2.2 copy-start.10
  118.7 26.4 %copy-start.23 = (f32[64,192]{1,0:T(8,128)S(1)}, f32[64,192]{1,0:T(8,128)}, u32[]{:S(2)}) copy-start(f32[64,192]{1,0:T(8,128)} %copy-done.22) | copy-start | bytes 147460
  142.2 2.9 %copy-start.13 = (f32[128,384]{1,0:T(8,128)S(1)}, f32[128,384]{1,0:T(8,128)}, u32[]{:S(2)}) copy-start(f32[128,384]{1,0:T(8,128)} %shard_map.218) | copy-start | bytes 589828
  156.5 1.8 copy-start.9
  157.2 2.7 %copy-start.24 = (bf16[576,192]{1,0:T(8,128)(2,1)S(1)}, bf16[576,192]{1,0:T(8,128)(2,1)}, u32[]{:S(2)}) copy-start(bf16[576,192]{1,0:T(8,128)(2,1)} %get-tuple-element.32) | copy-start | bytes 663556
  157.2 2.7 %copy-start.30 = (f32[576]{0:T(1024)S(1)}, f32[576]{0:T(1024)}, u32[]{:S(2)}) copy-start(f32[576]{0:T(1024)} %copy-done.29) | copy-start | bytes 6916
  157.2 2.8 %copy-start.34 = (f32[2,64]{1,0:T(2,128)S(1)}, f32[2,64]{1,0:T(2,128)}, u32[]{:S(2)}) copy-start(f32[2,64]{1,0:T(2,128)} %copy-done.33) | copy-start | bytes 1540
  158.3 2.1 copy-start.17
  158.3 2.1 copy-start.32
  158.3 2.1 copy-start.36
  158.3 2.1 copy-start.39
  160.0 2.0 copy-start.25
  252.1 1.7 copy-start.18
  255.7 3.1 %copy-start.1 = (bf16[768,576]{0,1:T(8,128)(2,1)S(1)}, bf16[768,576]{0,1:T(8,128)(2,1)}, u32[]{:S(2)}) copy-start(bf16[768,576]{0,1:T(8,128)(2,1)} %param.22) | copy-start | bytes 2654212
  (8 other events, 9.4 us)

commit v3 on v2

--- a/solution.py
+++ b/solution.py
@@ -686,7 +686,7 @@
         4,
         ((("core", "x"), False),),
         (kv_back.reshape(2, 2, members, rows, 2 * KV_WIDTH),),
-        rows // 2,
+        rows // 4,
     )
     query_grad_r = (
         rotary_inverse(
@@ -736,7 +736,7 @@
         5,
         ((("core", "y", "x"), True),) + ((("core", "x"), True),) * 3,
         (jnp.stack(sides, axis=1), gate_wgrad, up_wgrad, down_wgrad),
-        32,
+        16,
         small,
     )
     flat = unchunk(attn_total, count)

time: 260 us -> 269 us (1.035)
  Pallas kernels: 167 us -> 176 us
    pallas_call x2, Pallas kernels: 103 us -> 112 us  [reduce_chunks(): pl.pallas_call(functools.partial(reduce_kernel, members, kinds, tuple(flo...]
where the time goes in v3:
time: 269 us; the launch traced here: 268 us
  Pallas kernels  176 us (65%)
  local copies, waits for them, and re-layouts  46.6 us (17%)
  other arithmetic  19.9 us (7%)
  matrix products  18.9 us (7%)
  between operations  6.88 us (3%)
    pallas_call x2, Pallas kernels, reduce_chunks(): pl.pallas_call(functools.partial(reduce_kernel, members, kinds, tuple(flo...  112 us
    pallas_call x1, Pallas kernels, gather_keys(): pl.pallas_call(functools.partial(keys_kernel, members), out_shape=[jax.Sh...  21.7 us
    pallas_call x2, Pallas kernels, swap_rows(): pl.pallas_call(functools.partial(swap_kernel, members, count), out_shape=...  17.4 us
    pallas_call x1, Pallas kernels, gather_weights(): pl.pallas_call(functools.partial(weights_kernel, members, count), out_sha...  14.7 us
    unnamed x88, local copies, waits for them, and re-layouts  7.06 us
    dot_general x5, matrix products, outer_sum(): lax.dot_general(flat_left, flat_right, (((0,), (0,)), ((), ())), preferre...  6.29 us
    dot_general x7, matrix products, back_dot(): lax.dot_general(grads, weight, (((grads.ndim - 1,), (1,)), ((), ())), pre...  5.82 us
    pallas_call x1, Pallas kernels, attend_back(): pl.pallas_call(functools.partial(attend_back_kernel, window, block), out_...  5.54 us

profile of v3, /device:TPU:1, one launch (start us, length us, event | category | flops | bytes accessed | tf_op | source)
XLA Modules:
  0.0 267.9 jit_solution(1204162198008437611)
XLA Ops:
  7.2 1.3 fusion.51
  18.6 14.7 %shard_map.212 = (bf16[576,576]{1,0:T(8,128)(2,1)}, bf16[576,192]{1,0:T(8,128)(2,1)}, bf16[576,192]{1,0:T(8,128)(2,1)}, f32[2,8,288]{2,1,0:T(8,128)}) custom-call(bf16[288,576]{1,0:T(8,128)(2,1)} %refs_0_.1, bf16[288,192]{1,0:T(8,128)(2,1)} %refs_1_.1, bf16[288,192]{1,0:T(8,128)(2,1)} %refs_2_.1, f32[8,288]{1,0:T(8,128)} %fusion.43.refs_3_), custom_call_target="tpu_custom_call" | custom-call | tf_op jit(solution)/shard_map/pallas_call | solution.py:125
  38.5 1.2 reshape.216
  42.1 2.0 fusion.17
  45.4 21.7 %shard_map.213 = (bf16[2,2,4,4,32,384]{5,4,3,2,1,0:T(8,128)(2,1)}, bf16[128,576]{1,0:T(8,128)(2,1)}, bf16[576,576]{1,0:T(8,128)(2,1)}) custom-call(bf16[4,32,384]{2,1,0:T(8,128)(2,1)} %pad_maximum_fusion.10.kv_ref, bf16[128,576]{1,0:T(8,128)(2,1)} %bitcast.120, bf16[288,576]{1,0:T(8,128)(2,1)} %w_ref.1), custom_call_target="tpu_custom_call" | custom-call | tf_op jit(solution)/shard_map/pallas_call | solution.py:179
  67.1 4.1 %shard_map.214 = (f32[4,3,32,384]{3,2,1,0:T(8,128)}, f32[4,288,1]{2,1,0:T(8,128)}) custom-call(s32[20]{0:T(128)} %pad_add_fusion.1.slot_ref, bf16[4,3,32,384]{3,2,1,0:T(8,128)(2,1)} %pad.29.q_ref, bf16[16,4,32,384]{3,2,1,0:T(8,128)(2,1)} %bitcast.108, f32[4,32,160]{2,1,0:T(8,128)} %bitcast.138), custom_call_target="tpu_custom_call" | custom-call | tf_op jit(solution)/shard_map/pallas_call | solution.py:432
  74.1 1.6 multiply_reduce_fusion.2
  76.5 7.3 %shard_map.215 = bf16[128,576]{1,0:T(8,128)(2,1)} custom-call(bf16[128,576]{1,0:T(8,128)(2,1)} %bitcast.110), custom_call_target="tpu_custom_call" | custom-call | tf_op jit(solution)/shard_map/pallas_call | solution.py:206
  83.8 1.5 fusion.55
  85.9 1.5 multiply_convert_fusion
  90.4 1.6 convolution_convert_fusion
  92.0 1.5 copy.170
  93.5 1.5 fusion.67
  96.3 10.1 %shard_map.216 = (bf16[128,576]{1,0:T(8,128)(2,1)}, bf16[128,576]{1,0:T(8,128)(2,1)}) custom-call(bf16[128,576]{1,0:T(8,128)(2,1)} %copy.189.refs_0_, bf16[128,576]{1,0:T(8,128)(2,1)} %copy.192.refs_1_), custom_call_target="tpu_custom_call" | custom-call | tf_op jit(solution)/shard_map/pallas_call | solution.py:206
  106.4 1.7 convert_add_fusion.1
  112.2 5.5 %shard_map.217 = (f32[4,3,32,384]{3,2,1,0:T(8,128)}, bf16[16,4,32,384]{3,2,1,0:T(8,128)(2,1)}) custom-call(s32[20]{0:T(128)} %pad_add_fusion.1.slot_ref, bf16[4,3,32,384]{3,2,1,0:T(8,128)(2,1)} %pad.29.q_ref, bf16[16,4,32,384]{3,2,1,0:T(8,128)(2,1)} %bitcast.109, f32[4,32,160]{2,1,0:T(8,128)} %bitcast.139, bf16[4,3,32,384]{3,2,1,0:T(8,128)(2,1)} %pad.31.grad_ref, ...), custom_call_target="tpu_custom_call" | custom-call | tf_op jit(solution)/shard_map/pallas_call | solution.py:475
  118.8 23.9 %shard_map.218 = f32[128,384]{1,0:T(8,128)} custom-call(bf16[2,2,4,128,384]{4,3,2,1,0:T(8,128)(2,1)} %bitcast.132), custom_call_target="tpu_custom_call" | custom-call | tf_op jit(solution)/shard_map/pallas_call | solution.py:361
  142.7 1.7 slice.195
  146.2 1.3 convolution_convert_fusion.3
  147.4 1.4 convolution_convert_fusion.1
  148.9 1.3 copy.169
  150.2 1.4 convolution_convert_fusion.2
  151.7 1.3 copy.168
  165.1 1.6 pad_maximum_fusion.refs_0_
  166.7 88.3 %shard_map.219 = (bf16[2,2,4,48,576]{4,3,2,1,0:T(8,128)(2,1)}, bf16[2,2,4,48,576]{4,3,2,1,0:T(8,128)(2,1)}, bf16[2,2,4,48,576]{4,3,2,1,0:T(8,128)(2,1)}, bf16[2,2,4,48,576]{4,3,2,1,0:T(8,128)(2,1)}, f32[8,576]{1,0:T(8,128)}) custom-call(bf16[2,2,2,4,48,576]{5,4,3,2,1,0:T(8,128)(2,1)} %pad_maximum_fusion.refs_0_, bf16[2,2,4,48,576]{4,3,2,1,0:T(8,128)(2,1)} %bitcast.117, ...), custom_call_target="tpu_custom_call" | custom-call | tf_op jit(solution)/shard_map/pallas_call | solution.py:361
  255.0 1.5 dynamic-slice_reduce_fusion
  256.4 1.5 fusion.61
  259.5 1.3 fusion.58
  261.1 1.7 copy.173
  263.0 1.7 copy.174
  264.7 1.4 bitcast_convert_fusion.1
  266.1 1.7 copy.175
  (199 shorter events, 49.1 us)
Async XLA Ops:
  0.6 85.2 %copy-start = (bf16[768,576]{0,1:T(8,128)(2,1)S(1)}, bf16[768,576]{0,1:T(8,128)(2,1)}, u32[]{:S(2)}) copy-start(bf16[768,576]{0,1:T(8,128)(2,1)} %param.22) | copy-start | bytes 2654212
  0.7 33.7 %copy-start.2 = (bf16[2,64,576]{2,1,0:T(8,128)(2,1)S(1)}, bf16[2,64,576]{2,1,0:T(8,128)(2,1)}, u32[]{:S(2)}) copy-start(bf16[2,64,576]{2,1,0:T(8,128)(2,1)} %param.13) | copy-start | bytes 442372
  9.6 28.2 %copy-start.33 = (f32[2,64]{1,0:T(2,128)}, f32[2,64]{1,0:T(2,128)S(1)}, u32[]{:S(2)}) copy-start(f32[2,64]{1,0:T(2,128)S(1)} %add_rsqrt_fusion.1) | copy-start | bytes 1540
  17.0 20.1 %copy-start.22 = (f32[64,192]{1,0:T(8,128)}, f32[64,192]{1,0:T(8,128)S(1)}, u32[]{:S(2)}) copy-start(f32[64,192]{1,0:T(8,128)S(1)} %copy.142) | copy-start | bytes 147460
  33.3 4.5 %copy-start.8 = (bf16[576,576]{1,0:T(8,128)(2,1)S(1)}, bf16[576,576]{1,0:T(8,128)(2,1)}, u32[]{:S(2)}) copy-start(bf16[576,576]{1,0:T(8,128)(2,1)} %get-tuple-element.30) | copy-start | bytes 1990660
  34.2 75.8 %copy-start.31 = (f32[576]{0:T(1024)}, f32[576]{0:T(1024)S(1)}, u32[]{:S(2)}) copy-start(f32[576]{0:T(1024)S(1)} %mul.287) | copy-start | bytes 6916
  34.3 3.9 %copy-start.29 = (f32[576]{0:T(1024)}, f32[576]{0:T(1024)S(1)}, u32[]{:S(2)}) copy-start(f32[576]{0:T(1024)S(1)} %mul.259) | copy-start | bytes 6916
  40.5 1.7 copy-start.26
  40.5 1.7 copy-start.27
  72.8 11.0 %copy-start.6 = (bf16[576,768]{1,0:T(8,128)(2,1)S(1)}, bf16[576,768]{1,0:T(8,128)(2,1)}, u32[]{:S(2)}) copy-start(bf16[576,768]{1,0:T(8,128)(2,1)} %param.21) | copy-start | bytes 2654212
  74.1 11.3 %copy-start.5 = (bf16[576,768]{1,0:T(8,128)(2,1)S(1)}, bf16[576,768]{1,0:T(8,128)(2,1)}, u32[]{:S(2)}) copy-start(bf16[576,768]{1,0:T(8,128)(2,1)} %param.20) | copy-start | bytes 2654212
  75.7 34.4 %copy-start.35 = (f32[2,64]{1,0:T(2,128)}, f32[2,64]{1,0:T(2,128)S(1)}, u32[]{:S(2)}) copy-start(f32[2,64]{1,0:T(2,128)S(1)} %add_rsqrt_fusion) | copy-start | bytes 1540
  76.5 8.9 %copy-start.3 = (bf16[2,64,576]{2,1,0:T(8,128)(2,1)S(1)}, bf16[2,64,576]{2,1,0:T(8,128)(2,1)}, u32[]{:S(2)}) copy-start(bf16[2,64,576]{2,1,0:T(8,128)(2,1)} %multiply_convert_fusion.3) | copy-start | bytes 442372
  83.8 1.6 copy-start.4
  83.8 2.1 copy-start.11
  83.8 2.1 copy-start.28
  95.0 11.4 %copy-start.16 = (f32[128,576]{1,0:T(8,128)S(1)}, f32[128,576]{1,0:T(8,128)}, u32[]{:S(2)}) copy-start(f32[128,576]{1,0:T(8,128)} %copy.188) | copy-start | bytes 884740
  96.3 13.7 %copy-start.12 = (bf16[2,64,576]{2,1,0:T(8,128)(2,1)S(1)}, bf16[2,64,576]{2,1,0:T(8,128)(2,1)}, u32[]{:S(2)}) copy-start(bf16[2,64,576]{2,1,0:T(8,128)(2,1)} %param.25) | copy-start | bytes 442372
  108.0 2.2 copy-start.10
  118.8 26.8 %copy-start.23 = (f32[64,192]{1,0:T(8,128)S(1)}, f32[64,192]{1,0:T(8,128)}, u32[]{:S(2)}) copy-start(f32[64,192]{1,0:T(8,128)} %copy-done.22) | copy-start | bytes 147460
  142.7 2.9 %copy-start.13 = (f32[128,384]{1,0:T(8,128)S(1)}, f32[128,384]{1,0:T(8,128)}, u32[]{:S(2)}) copy-start(f32[128,384]{1,0:T(8,128)} %shard_map.218) | copy-start | bytes 589828
  157.0 1.8 copy-start.9
  157.7 2.7 %copy-start.24 = (bf16[576,192]{1,0:T(8,128)(2,1)S(1)}, bf16[576,192]{1,0:T(8,128)(2,1)}, u32[]{:S(2)}) copy-start(bf16[576,192]{1,0:T(8,128)(2,1)} %get-tuple-element.32) | copy-start | bytes 663556
  157.7 2.8 %copy-start.30 = (f32[576]{0:T(1024)S(1)}, f32[576]{0:T(1024)}, u32[]{:S(2)}) copy-start(f32[576]{0:T(1024)} %copy-done.29) | copy-start | bytes 6916
  157.7 2.8 %copy-start.34 = (f32[2,64]{1,0:T(2,128)S(1)}, f32[2,64]{1,0:T(2,128)}, u32[]{:S(2)}) copy-start(f32[2,64]{1,0:T(2,128)} %copy-done.33) | copy-start | bytes 1540
  158.7 2.1 copy-start.17
  158.8 2.1 copy-start.32
  158.8 2.1 copy-start.36
  158.8 2.1 copy-start.39
  160.5 2.0 copy-start.25
  261.1 1.7 copy-start.18
  264.7 3.1 %copy-start.1 = (bf16[768,576]{0,1:T(8,128)(2,1)S(1)}, bf16[768,576]{0,1:T(8,128)(2,1)}, u32[]{:S(2)}) copy-start(bf16[768,576]{0,1:T(8,128)(2,1)} %param.22) | copy-start | bytes 2654212
  (8 other events, 9.4 us)
